TPU v7x, 32 devices: a whole 2x2x4 slice. The times are simulated.
32 devices in a mesh: groups: 2 (over x), expert: 16 (over z, y, core), tensor: 1.
Axes of the slice: x: 2, y: 2, z: 4, core: 2. Of those that a mesh axis runs over, the one named last changes fastest.
Arguments:
- queries: bfloat16 [2048, 64, 288], P(('groups', 'expert'), 'tensor'), parts along dimension 0, may hold values from -64 to 64
- kv_latent: bfloat16 [2048, 288], P(('groups', 'expert')), parts along dimension 0, may hold values from -5 to 5
- value_up: bfloat16 [64, 256, 128], P('tensor', 'expert'), may hold values from -0.375 to 0.375
- out_proj: bfloat16 [8192, 3584], P('tensor', 'expert'), may hold values from -0.0625 to 0.0625
- norm_gain: float32 [3584], replicated, may hold values from 0.25 to 1.75
- gate_proj: bfloat16 [16, 3584, 1024], P('expert', None, 'tensor'), may hold values from -0.09375 to 0.09375
- up_proj: bfloat16 [16, 3584, 1024], P('expert', None, 'tensor'), may hold values from -0.09375 to 0.09375
- down_proj: bfloat16 [16, 1024, 3584], P('expert', 'tensor'), may hold values from -0.1875 to 0.1875
- routes: int32 [2048, 8], P(('groups', 'expert', 'tensor')), parts along dimension 0, may hold values from 0 to 15, all different within a row; in each aligned block of 64 rows (0 to 63, 64 to 127, ...) at most 40 rows name the same one
- route_weights: float32 [2048, 8], P(('groups', 'expert', 'tensor')), parts along dimension 0, may hold values from 0.05 to 0.6
Outputs:
- layer_out: bfloat16 [2048, 3584], P(('groups', 'expert', 'tensor')), parts along dimension 0
There are 2 independent parts, one for each index of `groups`. A program takes and returns all parts, laid end to end along the dimension named above; an argument that names none is the same for every part. Nothing has to cross between parts.
Inputs may be any that keep to these rules, and one draw needn't show every extreme that they name: `routes`: the tokens of one device (aligned blocks of 64 rows) name no expert more than 40 times; each token names 8 different experts.
All inputs are finite; a program needn't handle non-finite values.
Results may differ from a plain program's by a relative error of at most 0.029.
Values may be sent and summed in bfloat16 or wider, within the bound.
No kernel may reach another device: no remote copies, remote signals or barrier semaphores. Data moves between devices by JAX's collectives and lax.ppermute only.
A program may use at most 128 MiB of HBM per device.

v0:
```python
import jax
import jax.numpy as jnp
from jax import lax
from jax.sharding import PartitionSpec as P

LAT = 256
VD = 128
TOP = 8


score_scale = 0.0722


def local(
    queries,
    kv_latent,
    value_up,
    out_proj,
    norm_gain,
    gate_proj,
    up_proj,
    down_proj,
    routes,
    route_weights,
):
    tok, heads, width = queries.shape
    query_place = lax.axis_index("expert") * tok + jnp.arange(tok)
    piece = lax.all_gather(kv_latent, "expert", axis=0, tiled=True)
    running = jnp.full((tok, heads), -1e30, jnp.float32)
    count = piece.shape[0]
    scores = (
        jnp.einsum("shc,tc->sht", queries, piece, preferred_element_type=jnp.float32) * score_scale
    )
    key_place = jnp.arange(count)
    allowed = (query_place[:, None] >= key_place[None, :])[:, None, :]
    scores = jnp.where(allowed, scores, -1e30)
    newer = jnp.maximum(running, jnp.max(scores, axis=-1))
    expo = jnp.where(allowed, jnp.exp(scores - newer[..., None]), 0.0)
    total = jnp.sum(expo, axis=-1)
    update = jnp.einsum(
        "sht,tc->shc", expo.astype(jnp.bfloat16), piece[:, :LAT], preferred_element_type=jnp.float32
    )
    running, total, acc = (newer, total, update)
    latent_out = (acc / total[..., None]).astype(jnp.bfloat16)
    lifted = jnp.einsum(
        "shc,hcv->shv",
        latent_out,
        lax.all_gather(value_up, "expert", axis=1, tiled=True),
        preferred_element_type=jnp.float32,
    )
    flat_heads = lifted.astype(jnp.bfloat16).reshape(tok, heads * VD)
    partial_cols = jnp.dot(
        lax.all_gather(flat_heads, "expert", axis=0, tiled=True),
        out_proj,
        preferred_element_type=jnp.float32,
    )
    wide_rows = lax.all_to_all(
        partial_cols.astype(jnp.bfloat16), "expert", split_axis=0, concat_axis=1, tiled=True
    ).astype(partial_cols.dtype)
    attn = lax.psum_scatter(
        wide_rows.astype(jnp.bfloat16), "tensor", scatter_dimension=0, tiled=True
    )
    attn32 = attn.astype(jnp.float32)
    scale = lax.rsqrt(jnp.mean(attn32 * attn32, axis=-1, keepdims=True) + 1e-06)
    normed = (attn32 * scale * norm_gain).astype(jnp.bfloat16)
    rows = routes.shape[0]
    experts = lax.axis_size("expert") * gate_proj.shape[0]
    capacity = min(rows, max(2, 5 * rows * TOP // (4 * experts)))
    width_d = normed.shape[1]
    flat_routes = routes.reshape(-1)
    onehot = (flat_routes[:, None] == jnp.arange(experts)[None, :]).astype(jnp.int32)
    before = jnp.cumsum(onehot, axis=0) - onehot
    slot = jnp.sum(before * onehot, axis=1).reshape(rows, TOP)
    target = routes * capacity + slot
    slot_ids = jnp.arange(experts * capacity)
    placing = jnp.sum(
        (target[None, :, :] == slot_ids[:, None, None]).astype(jnp.int32), axis=2
    ).astype(jnp.bfloat16)
    outbound = jnp.dot(placing, normed, preferred_element_type=jnp.float32).astype(jnp.bfloat16)
    arrived = lax.all_to_all(
        outbound.reshape(experts, capacity, width_d),
        "expert",
        split_axis=0,
        concat_axis=0,
        tiled=True,
    )
    both_halves = lax.all_gather(arrived, "tensor", axis=0, tiled=True).reshape(-1, width_d)
    gate = jnp.dot(both_halves, gate_proj[0], preferred_element_type=jnp.float32)
    upper = jnp.dot(both_halves, up_proj[0], preferred_element_type=jnp.float32)
    hidden = (jax.nn.silu(gate) * upper).astype(jnp.bfloat16)
    down_terms = jnp.dot(hidden, down_proj[0], preferred_element_type=jnp.float32)
    expert_out = lax.psum_scatter(
        down_terms.astype(jnp.bfloat16), "tensor", scatter_dimension=0, tiled=True
    )
    back = lax.all_to_all(
        expert_out.reshape(experts, capacity, width_d),
        "expert",
        split_axis=0,
        concat_axis=0,
        tiled=True,
    )
    picked = back.reshape(-1, width_d)[target]
    mixed = jnp.sum(route_weights[:, :, None] * picked.astype(jnp.float32), axis=1)
    return (attn32 + mixed).astype(jnp.bfloat16)


def solution(mesh):
    in_specs = (
        P(("groups", "expert"), "tensor", None),
        P(("groups", "expert"), None),
        P("tensor", "expert", None),
        P("tensor", "expert"),
        P(),
        P("expert", None, "tensor"),
        P("expert", None, "tensor"),
        P("expert", "tensor", None),
        P(("groups", "expert", "tensor"), None),
        P(("groups", "expert", "tensor"), None),
    )
    out_specs = P(("groups", "expert", "tensor"), None)
    return jax.shard_map(local, mesh=mesh, in_specs=in_specs, out_specs=out_specs, check_vma=False)
```

profile of v0, /device:TPU:13, one launch (start us, length us, event | category | flops | bytes accessed | tf_op | source)
XLA Modules:
  0.0 501.2 jit_solution(149975867564121589)
XLA Ops:
  6.5 0.7 all-gather.3.cloned.1.call-update
  7.4 19.3 %all_gather.10 = bf16[1024,288]{1,0:T(8,128)(2,1)S(1)} all-gather(bf16[64,288]{1,0:T(8,128)(2,1)} %param.11), channel_id=1, replica_groups=mesh['groups'=2,'expert'=16,'tensor'=1] {'expert'}, dimensions={0}, use_global_device_ids=true | all-gather | bytes 626688 | tf_op jit(solution)/shard_map/all_gather | solution.py:28
  26.7 5.7 %fusion = (f32[64,64]{1,0:T(8,128)S(1)}, f32[64,64,1024]{2,1,0:T(8,128)S(1)}) fusion(pred[64,1024]{1,0:T(8,128)(4,1)S(1)} %iota_compare_fusion.1, bf16[64,64,288]{2,1,0:T(8,128)(2,1)S(1)} %copy-done, bf16[1024,288]{1,0:T(8,128)(2,1)S(1)} %all_gather.10), kind=kOutput, calls=%fused_computation.3 | convolution fusion | flops 2428497920 | bytes 19808256 | tf_op jit(solution)/shard_map/shc,tc->sht/dot_general | solution.py:32
  32.5 7.6 %fusion.2 = (bf16[64,64,1024]{2,1,0:T(8,128)(2,1)}, f32[64,64]{1,0:T(8,128)S(1)}) fusion(f32[64,64,1024]{2,1,0:T(8,128)S(1)} %get-tuple-element.10, f32[64,64]{1,0:T(8,128)S(1)} %broadcast_maximum_fusion, pred[64,1024]{1,0:T(8,128)(4,1)S(1)} %iota_compare_fusion.1), kind=kLoop, calls=%fused_computation.5 | loop fusion | flops 25161728 | bytes 25264128 | tf_op jit(solution)/shard_map/convert_element_type | solution.py:41
  40.1 23.7 %all-gather.3.cloned.1.call-done = bf16[64,256,128]{2,1,0:T(8,128)(2,1)} async-done(((bf16[64,16,128]{2,1,0:T(8,128)(2,1)}), bf16[64,256,128]{2,1,0:T(8,128)(2,1)}) %all-gather.3.cloned.1.call-update) | async-done | bytes 4194320 | tf_op jit(solution)/shard_map/all_gather | solution.py:48
  63.8 13.9 %fusion.21 = bf16[64,8,8,128]{3,2,1,0:T(8,128)(2,1)S(1)} fusion(bf16[64,256,128]{2,1,0:T(8,128)(2,1)} %all-gather.3.cloned.1.call-done, f32[64,64]{0,1:T(8,128)S(1)} %copy.55, bf16[64,64,1024]{2,1,0:T(8,128)(2,1)} %get-tuple-element.7, bf16[1024,288]{1,0:T(8,128)(2,1)S(1)} %copy-done.6), kind=kOutput, calls=%fused_computation.22 | convolution fusion | flops 2418540544 | bytes 14188544 | tf_op jit(solution)/shard_map/shc,hcv->shv/dot_general | solution.py:45
  77.7 1.2 copy.76
  78.9 125.0 %all-gather.5.cloned.1.call-done = bf16[1024,8192]{1,0:T(8,128)(2,1)} async-done(((bf16[64,8192]{1,0:T(8,128)(2,1)}), bf16[1024,8192]{1,0:T(8,128)(2,1)}) %all-gather.5.cloned.1.call-update) | async-done | bytes 16777232 | tf_op jit(solution)/shard_map/all_gather | solution.py:53
  204.0 12.1 %convolution_convert_fusion.1 = bf16[1024,224]{0,1:T(8,128)(2,1)S(1)} fusion(bf16[1024,8192]{1,0:T(8,128)(2,1)} %all-gather.5.cloned.1.call-done, bf16[8192,224]{0,1:T(8,128)(2,1)} %param.13), kind=kOutput, calls=%fused_computation.28 | convolution fusion | flops 3758325760 | bytes 20905984 | tf_op jit(solution)/shard_map/dot_general | solution.py:52
  216.1 1.0 copy.57
  217.1 6.7 %all-to-all-start = ((bf16[16,64,224]{2,1,0:T(8,128)(2,1)}), bf16[16,64,224]{2,1,0:T(8,128)(2,1)S(1)}, u32[]{:S(2)}, u32[]{:S(2)}) async-start(bf16[16,64,224]{2,1,0:T(8,128)(2,1)} %bitcast.3), calls=%async_computation | async-start | bytes 1048576 | tf_op jit(solution)/shard_map/all_to_all | solution.py:57
  224.0 1.2 reduce-window.6
  226.3 11.1 %all-to-all-done = bf16[16,64,224]{2,1,0:T(8,128)(2,1)S(1)} async-done(((bf16[16,64,224]{2,1,0:T(8,128)(2,1)}), bf16[16,64,224]{2,1,0:T(8,128)(2,1)S(1)}, u32[]{:S(2)}, u32[]{:S(2)}) %all-to-all-start) | async-done | bytes 458784 | tf_op jit(solution)/shard_map/all_to_all | solution.py:57
  238.1 0.6 reshape.83
  239.0 1.4 convolution_convert_fusion
  240.4 105.9 %all_to_all.23 = bf16[16,40,3584]{2,1,0:T(8,128)(2,1)S(1)} all-to-all(bf16[16,40,3584]{2,1,0:T(8,128)(2,1)S(1)} %bitcast.65), channel_id=1, replica_groups=mesh['groups'=2,'expert'=16,'tensor'=1] {'expert'}, dimensions={0} | all-to-all | bytes 9175040 | tf_op jit(solution)/shard_map/all_to_all | solution.py:80
  346.3 2.1 copy-done.4
  348.4 4.9 fusion.10
  353.3 17.3 %fusion.12 = bf16[640,3584]{1,0:T(8,128)(2,1)} fusion(bf16[1,1024,3584]{2,1,0:T(8,128)(2,1)} %param.17, f32[640,1024]{1,0:T(8,128)S(1)} %fusion.10, bf16[640,3584]{1,0:T(8,128)(2,1)} %bitcast.68, bf16[1,3584,1024]{2,1,0:T(8,128)(2,1)} %param.16), kind=kOutput, calls=%fused_computation.16 | convolution fusion | flops 9401466880 | bytes 26476544 | tf_op jit(solution)/shard_map/dot_general | solution.py:91
  370.6 5.9 %all-to-all-start.2 = ((bf16[16,40,3584]{2,1,0:T(8,128)(2,1)}), bf16[16,40,3584]{2,1,0:T(8,128)(2,1)}, u32[]{:S(2)}, u32[]{:S(2)}) async-start(bf16[16,40,3584]{2,1,0:T(8,128)(2,1)} %bitcast.66), calls=%async_computation.2 | async-start | bytes 9175040 | tf_op jit(solution)/shard_map/all_to_all | solution.py:95
  376.7 100.5 %all-to-all-done.2 = bf16[16,40,3584]{2,1,0:T(8,128)(2,1)} async-done(((bf16[16,40,3584]{2,1,0:T(8,128)(2,1)}), bf16[16,40,3584]{2,1,0:T(8,128)(2,1)}, u32[]{:S(2)}, u32[]{:S(2)}) %all-to-all-start.2) | async-done | bytes 4587552 | tf_op jit(solution)/shard_map/all_to_all | solution.py:95
  477.2 10.9 %gather_fusion = bf16[512,3584]{1,0:T(8,128)(2,1)} fusion(bf16[640,3584]{1,0:T(8,128)(2,1)} %bitcast.12, s32[1024]{0:T(1024)S(1)} %pad_clamp_fusion), kind=kCustom, calls=%fused_computation | custom fusion | bytes 7342080 | tf_op jit(solution)/shard_map/gather | solution.py:102
  488.1 5.1 %fusion.5 = f32[64,3584]{1,0:T(8,128)S(1)} fusion(bf16[512,3584]{1,0:T(8,128)(2,1)} %gather_fusion, f32[64,8]{1,0:T(8,128)S(1)} %copy.59), kind=kLoop, calls=%fused_computation.9 | loop fusion | flops 5275648 | bytes 4589568 | tf_op jit(solution)/shard_map/reduce_sum | solution.py:103
  493.3 0.9 add_convert_fusion
  (52 shorter events, 2.9 us)
Async XLA Ops:
  6.5 20.2 %copy-start = (bf16[64,64,288]{2,1,0:T(8,128)(2,1)S(1)}, bf16[64,64,288]{2,1,0:T(8,128)(2,1)}, u32[]{:S(2)}) copy-start(bf16[64,64,288]{2,1,0:T(8,128)(2,1)} %param.10) | copy-start | bytes 7077892
  6.5 57.3 %all-gather.3.cloned.1.call-start = ((), (), s32[]{:S(2)}) async-start(), calls=%async_computation.3 | async-start | bytes 4456448 | tf_op jit(solution)/shard_map/all_gather | solution.py:48
  7.3 196.7 %all-gather.5.cloned.1.call-start = ((), (), s32[]{:S(2)}) async-start(), calls=%async_computation.4 | async-start | bytes 17825792 | tf_op jit(solution)/shard_map/all_gather | solution.py:53
  26.7 5.7 %copy-start.5 = (bf16[1024,288]{1,0:T(8,128)(2,1)}, bf16[1024,288]{1,0:T(8,128)(2,1)S(1)}, u32[]{:S(2)}) copy-start(bf16[1024,288]{1,0:T(8,128)(2,1)S(1)} %all_gather.10) | copy-start | bytes 1769476
  32.4 31.4 %copy-start.6 = (bf16[1024,288]{1,0:T(8,128)(2,1)S(1)}, bf16[1024,288]{1,0:T(8,128)(2,1)}, u32[]{:S(2)}) copy-start(bf16[1024,288]{1,0:T(8,128)(2,1)} %copy-done.5) | copy-start | bytes 1769476
  78.9 144.8 %copy-start.8 = (s32[64,8]{0,1:T(8,128)S(1)}, s32[64,8]{0,1:T(8,128)}, u32[]{:S(2)}) copy-start(s32[64,8]{0,1:T(8,128)} %param.18) | copy-start | bytes 6148
  216.1 22.9 %copy-start.7 = (f32[3584]{0:T(1024)S(1)}, f32[3584]{0:T(1024)}, u32[]{:S(2)}) copy-start(f32[3584]{0:T(1024)} %param.14) | copy-start | bytes 43012
  217.1 20.3 %all-to-all-start = ((bf16[16,64,224]{2,1,0:T(8,128)(2,1)}), bf16[16,64,224]{2,1,0:T(8,128)(2,1)S(1)}, u32[]{:S(2)}, u32[]{:S(2)}) async-start(bf16[16,64,224]{2,1,0:T(8,128)(2,1)} %bitcast.3), calls=%async_computation | async-start | bytes 1048576 | tf_op jit(solution)/shard_map/all_to_all | solution.py:57
  238.7 107.6 %copy-start.2 = (f32[64,3584]{1,0:T(8,128)}, f32[64,3584]{1,0:T(8,128)S(1)}, u32[]{:S(2)}) copy-start(f32[64,3584]{1,0:T(8,128)S(1)} %reshape.83) | copy-start | bytes 2752516
  239.0 109.4 %slice-start = ((s8[7340032]{0:T(1024)(128)(4,1)}), s8[4194304]{0:T(1024)(128)(4,1)S(1)}, s32[]{:S(2)}) async-start(s8[7340032]{0:T(1024)(128)(4,1)} %bitcast.70), calls=%async_computation.5 | async-start | bytes 8388608
  240.4 108.0 %slice-start.1 = ((s8[7340032]{0:T(1024)(128)(4,1)}), s8[3145728]{0:T(1024)(128)(4,1)S(1)}, s32[]{:S(2)}) async-start(s8[7340032]{0:T(1024)(128)(4,1)} %bitcast.70), calls=%async_computation.6 | async-start | bytes 6291456
  346.3 2.1 copy-start.4
  370.6 6.0 %copy-start.9 = (f32[64,8]{0,1:T(8,128)S(1)}, f32[64,8]{0,1:T(8,128)}, u32[]{:S(2)}) copy-start(f32[64,8]{0,1:T(8,128)} %param.19) | copy-start | bytes 6148
  370.6 106.6 %all-to-all-start.2 = ((bf16[16,40,3584]{2,1,0:T(8,128)(2,1)}), bf16[16,40,3584]{2,1,0:T(8,128)(2,1)}, u32[]{:S(2)}, u32[]{:S(2)}) async-start(bf16[16,40,3584]{2,1,0:T(8,128)(2,1)} %bitcast.66), calls=%async_computation.2 | async-start | bytes 9175040 | tf_op jit(solution)/shard_map/all_to_all | solution.py:95
  477.2 16.9 %copy-start.1 = (bf16[64,64,288]{2,1,0:T(8,128)(2,1)S(1)}, bf16[64,64,288]{2,1,0:T(8,128)(2,1)}, u32[]{:S(2)}) copy-start(bf16[64,64,288]{2,1,0:T(8,128)(2,1)} %param.10) | copy-start | bytes 7077892
  488.1 5.1 %copy-start.3 = (f32[64,3584]{1,0:T(8,128)S(1)}, f32[64,3584]{1,0:T(8,128)}, u32[]{:S(2)}) copy-start(f32[64,3584]{1,0:T(8,128)} %copy-done.2) | copy-start | bytes 2752516
Sparse Core Ops, SparseCore 0:
  9.5 54.2 all-gather.2
  79.0 124.8 all-gather.4
where the time goes:
time: 507 us; the launch traced here: 501 us
  waiting for transfers between devices  261 us (51%)
  blocking collectives  125 us (25%)
  matrix products  55.3 us (11%)
  local copies, waits for them, and re-layouts  17.5 us (3%)
  other arithmetic  15.8 us (3%)
  between operations  13.9 us (3%)
  starting transfers between devices  12.6 us (2%)
    all_gather x1, waiting for transfers between devices, local(): lax.all_gather(flat_heads, 'expert', axis=0, tiled=True)  125 us
    all_to_all x1, blocking collectives, local(): lax.all_to_all(outbound.reshape(experts, capacity, width_d), 'expert', sp...  106 us
    all_to_all x1, waiting for transfers between devices, local(): lax.all_to_all(expert_out.reshape(experts, capacity, width_d), 'expert',...  100 us
    all_gather x1, waiting for transfers between devices, local(): lax.all_gather(value_up, 'expert', axis=1, tiled=True)  23.7 us
    all_gather x1, blocking collectives, local(): piece = lax.all_gather(kv_latent, 'expert', axis=0, tiled=True)  19.3 us
    dot_general x1, matrix products, local(): jnp.dot(hidden, down_proj[0], preferred_element_type=jnp.float32)  17.3 us
    dot_general x1, matrix products, local(): jnp.einsum('shc,hcv->shv', latent_out, lax.all_gather(value_up, 'expert',...  13.9 us
    dot_general x1, matrix products, local(): jnp.dot(lax.all_gather(flat_heads, 'expert', axis=0, tiled=True), out_pro...  12.1 us
  transfers between devices with their start and end apart: 4, of which 4 were waited for; matrix products, arithmetic and copies ran while one was open for 3% of the time, Pallas kernels for 0%

commit v1 on v0

--- a/solution.py
+++ b/solution.py
@@ -1,11 +1,12 @@
 import jax
 import jax.numpy as jnp
 from jax import lax
-from jax.sharding import PartitionSpec as P
+from jax.sharding import Mesh, PartitionSpec as P
 
 LAT = 256
 VD = 128
 TOP = 8
+NZ, NY, NC = 4, 2, 2
 
 
 score_scale = 0.0722
@@ -104,18 +105,145 @@
     return (attn32 + mixed).astype(jnp.bfloat16)
 
 
+def shift_z(value):
+    return lax.ppermute(value, "z", [(i, (i + 1) % NZ) for i in range(NZ)])
+
+
+def swap_y(value):
+    return lax.ppermute(value, "y", [(0, 1), (1, 0)])
+
+
+def swap_core(value):
+    return lax.ppermute(value, "core", [(0, 1), (1, 0)])
+
+
+def ring(block):
+    pieces = []
+    for r in range(NZ):
+        pieces.append((block, swap_y(block)))
+        if r < NZ - 1:
+            block = shift_z(block)
+    return pieces
+
+
+def boxed(
+    queries,
+    kv_latent,
+    value_up,
+    out_proj,
+    norm_gain,
+    gate_proj,
+    up_proj,
+    down_proj,
+    routes,
+    route_weights,
+):
+    f32, b16 = jnp.float32, jnp.bfloat16
+    tok, heads, width = queries.shape
+    z, y, core = (lax.axis_index(name) for name in ("z", "y", "core"))
+    place = (z * NY + y) * NC + core
+    experts = NZ * NY * NC
+    whole = ("z", "y", "core")
+
+    def origin(d, r, b):
+        return (((z - r) % NZ) * NY + (y ^ b)) * NC + (core ^ d)
+
+    dense = jnp.sum(
+        jnp.where(
+            routes[:, :, None] == jnp.arange(experts)[None, None, :], route_weights[:, :, None], 0.0
+        ),
+        axis=1,
+    )
+    keys = lax.all_gather(kv_latent, whole, axis=0, tiled=True)
+    dense_all = lax.all_gather(dense, whole, axis=0, tiled=True)
+
+    lift_rows = jnp.concatenate([p for pair in ring(value_up) for p in pair], axis=1)
+    lift = jnp.concatenate([lift_rows, swap_core(lift_rows)], axis=1)
+    part = value_up.shape[1]
+    order = jnp.stack([origin(d, r, b) for d in range(NC) for r in range(NZ) for b in range(NY)])
+    lat_order = (order[:, None] * part + jnp.arange(part)[None, :]).reshape(-1)
+    turn = (jnp.arange(LAT)[:, None] == lat_order[None, :]).astype(b16)
+    values = jnp.dot(keys[:, :LAT], turn, preferred_element_type=f32).astype(b16)
+    columns = jnp.concatenate([out_proj, swap_core(out_proj)], axis=1)
+
+    query_place = place * tok + jnp.arange(tok)
+    scores = jnp.einsum("shc,tc->sht", queries, keys, preferred_element_type=f32) * score_scale
+    allowed = (query_place[:, None] >= jnp.arange(keys.shape[0])[None, :])[:, None, :]
+    scores = jnp.where(allowed, scores, -1e30)
+    top = jnp.max(scores, axis=-1)
+    expo = jnp.where(allowed, jnp.exp(scores - top[..., None]), 0.0)
+    total = jnp.sum(expo, axis=-1)
+    acc = jnp.einsum("sht,tc->shc", expo.astype(b16), values, preferred_element_type=f32)
+    latent_out = (acc / total[..., None]).astype(b16)
+    lifted = jnp.einsum("shc,hcv->shv", latent_out, lift, preferred_element_type=f32)
+    flat_heads = lifted.astype(b16).reshape(tok, heads * VD)
+
+    strips = [
+        [jnp.dot(p, columns, preferred_element_type=f32).astype(b16) for p in pair]
+        for pair in ring(flat_heads)
+    ]
+    strips = jnp.stack([s for pair in strips for s in pair])
+    chips = NZ * NY
+    ids = jnp.arange(chips)
+    here = ((z - ids // NY) % NZ) * NY + (y ^ (ids % NY))
+    sent = jnp.take(strips, here, axis=0)
+    got = lax.all_to_all(sent, ("z", "y"), split_axis=0, concat_axis=0, tiled=True)
+    cols = out_proj.shape[1]
+    got = got.reshape(chips, tok, NC, cols)
+    got = jnp.where(core == 0, got, got[:, :, ::-1])
+    attn32 = jnp.transpose(got, (1, 0, 2, 3)).reshape(tok, -1).astype(f32)
+    scale = lax.rsqrt(jnp.mean(attn32 * attn32, axis=-1, keepdims=True) + 1e-06)
+    normed = (attn32 * scale * norm_gain).astype(b16)
+
+    width_d = normed.shape[1]
+    mine = jnp.take(dense_all, place, axis=1).reshape(experts, tok)
+    by_chunk = jnp.stack(
+        [origin(d, r, b) for r in range(NZ) for d in range(NC) for b in range(NY)]
+    )
+    shares = jnp.take(mine, by_chunk, axis=0).reshape(NZ, NC * NY * tok, 1)
+
+    def expert(block, share):
+        gate = jnp.dot(block, gate_proj[0], preferred_element_type=f32)
+        upper = jnp.dot(block, up_proj[0], preferred_element_type=f32)
+        hidden = (jax.nn.silu(gate) * upper).astype(b16)
+        return share * jnp.dot(hidden, down_proj[0], preferred_element_type=f32)
+
+    sums = []
+    for r, pair in enumerate(ring(normed)):
+        own = jnp.concatenate(pair, axis=0)
+        block = jnp.concatenate([own, swap_core(own)], axis=0)
+        out = expert(block, shares[r])
+        half = NY * tok
+        out = out[:half] + swap_core(out[half:].astype(b16)).astype(f32)
+        sums.append(out[:tok] + swap_y(out[tok:].astype(b16)).astype(f32))
+    acc = sums[1]
+    for r in (2, 3, 0):
+        acc = shift_z(acc.astype(b16)).astype(f32) + sums[r]
+    return (attn32 + acc).astype(b16)
+
+
 def solution(mesh):
+    names = "expert"
+    body = local
+    if mesh.shape["expert"] == NZ * NY * NC and mesh.shape["tensor"] == 1:
+        groups = mesh.shape["groups"]
+        mesh = Mesh(
+            mesh.devices.reshape(groups, NZ, NY, NC, 1), ("groups", "z", "y", "core", "tensor")
+        )
+        names = ("z", "y", "core")
+        body = boxed
+    every = ("groups",) + (names if isinstance(names, tuple) else (names,))
     in_specs = (
-        P(("groups", "expert"), "tensor", None),
-        P(("groups", "expert"), None),
-        P("tensor", "expert", None),
-        P("tensor", "expert"),
+        P(every, "tensor", None),
+        P(every, None),
+        P("tensor", names, None),
+        P("tensor", names),
         P(),
-        P("expert", None, "tensor"),
-        P("expert", None, "tensor"),
-        P("expert", "tensor", None),
-        P(("groups", "expert", "tensor"), None),
-        P(("groups", "expert", "tensor"), None),
-    )
-    out_specs = P(("groups", "expert", "tensor"), None)
-    return jax.shard_map(local, mesh=mesh, in_specs=in_specs, out_specs=out_specs, check_vma=False)
+        P(names, None, "tensor"),
+        P(names, None, "tensor"),
+        P(names, "tensor", None),
+        P(every + ("tensor",), None),
+        P(every + ("tensor",), None),
+    )
+    out_specs = P(every + ("tensor",), None)
+    return jax.shard_map(body, mesh=mesh, in_specs=in_specs, out_specs=out_specs, check_vma=False)

time: 507 us -> 453 us (0.89)
  the two profiles are of different devices: /device:TPU:13 before, /device:TPU:0 now
where the time goes in v1:
time: 453 us; the launch traced here: 446 us
  waiting for transfers between devices  171 us (38%)
  matrix products  120 us (26%)
  local copies, waits for them, and re-layouts  50.3 us (11%)
  blocking collectives  45.9 us (10%)
  other arithmetic  34.8 us (8%)
  starting transfers between devices  22.5 us (5%)
    ppermute x12, waiting for transfers between devices, shift_z(): return lax.ppermute(value, 'z', [(i, (i + 1) % NZ) for i in range(NZ)])  106 us
    ppermute x16, waiting for transfers between devices, swap_y(): return lax.ppermute(value, 'y', [(0, 1), (1, 0)])  54.3 us
    dot_general x4, matrix products, expert(): return share * jnp.dot(hidden, down_proj[0], preferred_element_type=f32)  47 us
    dot_general x8, matrix products, boxed(): jnp.dot(p, columns, preferred_element_type=f32).astype(b16)  26.1 us
    unnamed x73, local copies, waits for them, and re-layouts  24.2 us
    all_gather x1, blocking collectives, boxed(): keys = lax.all_gather(kv_latent, whole, axis=0, tiled=True)  23.8 us
    all_gather x1, blocking collectives, boxed(): dense_all = lax.all_gather(dense, whole, axis=0, tiled=True)  22.1 us
    sub x1, other arithmetic, boxed(): expo = jnp.where(allowed, jnp.exp(scores - top[..., None]), 0.0)  20.3 us
  transfers between devices with their start and end apart: 39, of which 18 were waited for; matrix products, arithmetic and copies ran while one was open for 41% of the time, Pallas kernels for 0%

profile of v1, /device:TPU:0, one launch (start us, length us, event | category | flops | bytes accessed | tf_op | source)
XLA Modules:
  0.0 446.2 jit_solution(1206416064959315622)
XLA Ops:
  4.6 23.8 %all_gather.6 = bf16[1024,288]{1,0:T(8,128)(2,1)S(1)} all-gather(bf16[64,288]{1,0:T(8,128)(2,1)} %param.11), channel_id=1, replica_groups=mesh['groups'=2,'z'=4,'y'=2,'core'=2,'tensor'=1] {'z','y','core'}, dimensions={0}, use_global_device_ids=true | all-gather | bytes 626688 | tf_op jit(solution)/shard_map/all_gather | solution.py:157
  28.3 8.1 %fusion.76 = f32[64,64,1024]{2,1,0:T(8,128)} fusion(bf16[64,64,288]{2,1,0:T(8,128)(2,1)S(1)} %copy-done, bf16[1024,288]{1,0:T(8,128)(2,1)S(1)} %all_gather.6), kind=kOutput, calls=%fused_computation.108 | convolution fusion | flops 2415919104 | bytes 19726336 | tf_op jit(solution)/shard_map/shc,tc->sht/dot_general | solution.py:170
  37.6 9.5 %collective-permute-done.3 = bf16[64,16,128]{2,1,0:T(8,128)(2,1)S(1)} collective-permute-done((bf16[64,16,128]{2,1,0:T(8,128)(2,1)}, bf16[64,16,128]{2,1,0:T(8,128)(2,1)S(1)}, u32[]{:S(2)}, u32[]{:S(2)}) %collective-permute-start.3) | collective-permute-done | bytes 262176 | tf_op jit(solution)/shard_map/ppermute | solution.py:109
  66.4 20.3 %fusion.124 = (bf16[64,64,1024]{2,1,0:T(8,128)(2,1)}, f32[64,64]{1,0:T(8,128)S(1)}) fusion(f32[64,64,1024]{2,1,0:T(8,128)} %fusion.76, pred[64,1024]{1,0:T(8,128)(4,1)S(1)} %iota_compare_fusion.1), kind=kOutput, calls=%fused_computation.201 | output fusion | flops 33555456 | bytes 25247744 | tf_op jit(solution)/shard_map/sub | solution.py:174
  95.3 14.0 %fusion.45 = bf16[64,8,8,128]{3,2,1,0:T(8,128)(2,1)S(1)} fusion(bf16[64,256,128]{2,1,0:T(8,128)(2,1)} %copy-done.25, f32[64,64]{0,1:T(8,128)S(1)} %copy.32, bf16[256,1024,1]{1,0,2:T(8,128)(2,1)S(1)} %copy-done.12, bf16[64,64,1024]{2,1,0:T(8,128)(2,1)} %get-tuple-element.16), kind=kOutput, calls=%fused_computation.51 | convolution fusion | flops 2418540544 | bytes 14172160 | tf_op jit(solution)/shard_map/shc,hcv->shv/dot_general | solution.py:178
  120.3 16.8 %collective-permute-done.10 = bf16[64,8192]{1,0:T(8,128)(2,1)S(1)} collective-permute-done((bf16[64,8192]{1,0:T(8,128)(2,1)S(1)}, bf16[64,8192]{1,0:T(8,128)(2,1)S(1)}, u32[]{:S(2)}, u32[]{:S(2)}) %collective-permute-start.10) | collective-permute-done | bytes 1048608 | tf_op jit(solution)/shard_map/ppermute | solution.py:109
  144.5 20.3 %collective-permute-done.12 = bf16[64,8192]{1,0:T(8,128)(2,1)S(1)} collective-permute-done((bf16[64,8192]{1,0:T(8,128)(2,1)S(1)}, bf16[64,8192]{1,0:T(8,128)(2,1)S(1)}, u32[]{:S(2)}, u32[]{:S(2)}) %collective-permute-start.12) | collective-permute-done | bytes 1048608 | tf_op jit(solution)/shard_map/ppermute | solution.py:109
  170.9 19.2 %collective-permute-done.14 = bf16[64,8192]{1,0:T(8,128)(2,1)S(1)} collective-permute-done((bf16[64,8192]{1,0:T(8,128)(2,1)S(1)}, bf16[64,8192]{1,0:T(8,128)(2,1)S(1)}, u32[]{:S(2)}, u32[]{:S(2)}) %collective-permute-start.14) | collective-permute-done | bytes 1048608 | tf_op jit(solution)/shard_map/ppermute | solution.py:109
  197.3 15.0 %collective-permute-done.15 = bf16[64,8192]{1,0:T(8,128)(2,1)S(1)} collective-permute-done((bf16[64,8192]{1,0:T(8,128)(2,1)S(1)}, bf16[64,8192]{1,0:T(8,128)(2,1)S(1)}, u32[]{:S(2)}, u32[]{:S(2)}) %collective-permute-start.15) | collective-permute-done | bytes 1048608 | tf_op jit(solution)/shard_map/ppermute | solution.py:113
  221.5 10.7 %all-to-all-done = bf16[8,64,448]{2,1,0:T(8,128)(2,1)S(1)} async-done(((bf16[8,64,448]{2,1,0:T(8,128)(2,1)}), bf16[8,64,448]{2,1,0:T(8,128)(2,1)S(1)}, u32[]{:S(2)}, u32[]{:S(2)}) %all-to-all-start) | async-done | bytes 458784 | tf_op jit(solution)/shard_map/all_to_all | solution.py:190
  241.1 22.1 %all-gather = f32[16,64,16]{1,2,0:T(8,128)S(1)} all-gather(f32[1,64,16]{1,2,0:T(8,128)S(1)} %bitcast.162), channel_id=1, replica_groups=mesh['groups'=2,'z'=4,'y'=2,'core'=2,'tensor'=1] {'z','y','core'}, dimensions={0}, use_global_device_ids=true | all-gather | bytes 69632 | tf_op jit(solution)/shard_map/all_gather | solution.py:158
  264.9 14.1 %collective-permute-done.16 = bf16[64,3584]{1,0:T(8,128)(2,1)S(1)} collective-permute-done((bf16[64,3584]{1,0:T(8,128)(2,1)S(1)}, bf16[64,3584]{1,0:T(8,128)(2,1)S(1)}, u32[]{:S(2)}, u32[]{:S(2)}) %collective-permute-start.16) | collective-permute-done | bytes 458784 | tf_op jit(solution)/shard_map/ppermute | solution.py:109
  279.1 11.9 %collective-permute-done.17 = bf16[64,3584]{1,0:T(8,128)(2,1)S(1)} collective-permute-done((bf16[64,3584]{1,0:T(8,128)(2,1)S(1)}, bf16[64,3584]{1,0:T(8,128)(2,1)S(1)}, u32[]{:S(2)}, u32[]{:S(2)}) %collective-permute-start.17) | collective-permute-done | bytes 458784 | tf_op jit(solution)/shard_map/ppermute | solution.py:113
  295.8 9.1 %collective-permute-done.23 = bf16[64,3584]{1,0:T(8,128)(2,1)S(1)} collective-permute-done((bf16[64,3584]{1,0:T(8,128)(2,1)S(1)}, bf16[64,3584]{1,0:T(8,128)(2,1)S(1)}, u32[]{:S(2)}, u32[]{:S(2)}) %collective-permute-start.23) | collective-permute-done | bytes 458784 | tf_op jit(solution)/shard_map/ppermute | solution.py:113
  306.9 6.5 %fusion.23 = f32[256,1024]{1,0:T(8,128)} fusion(bf16[1,3584,1024]{2,1,0:T(8,128)(2,1)} %param.15, bf16[128,3584]{1,0:T(8,128)(2,1)S(1)} %collective-permute-done.35, bf16[64,3584]{1,0:T(8,128)(2,1)} %copy-done.13, bf16[64,3584]{1,0:T(8,128)(2,1)S(1)} %copy-done.10), kind=kOutput, calls=%fused_computation.27 | convolution fusion | flops 1884553216 | bytes 10223616 | tf_op jit(solution)/shard_map/dot_general | solution.py:206
  313.4 11.7 %fusion.40 = f32[256,3584]{1,0:T(8,128)} fusion(bf16[1,1024,3584]{2,1,0:T(8,128)(2,1)} %param.17, f32[256]{0:T(256)S(1)} %mul.251, f32[256,1024]{1,0:T(8,128)} %fusion.23, bf16[1,3584,1024]{2,1,0:T(8,128)(2,1)} %param.16, bf16[128,3584]{1,0:T(8,128)(2,1)} %copy-done.28, bf16[64,3584]{1,0:T(8,128)(2,1)} %copy-done.13, bf16[64,3584]{1,0:T(8,128)(2,1)S(1)} %copy-done.11), kind=kOutput, calls=%fused_computation.38 | convolution fusion | flops 3766091776 | bytes 21234688 | tf_op jit(solution)/shard_map/dot_general | solution.py:209
  332.8 6.1 %fusion.21 = f32[256,1024]{1,0:T(8,128)} fusion(bf16[256,3584]{1,0:T(8,128)(2,1)S(1)} %constant_dynamic-update-slice_fusion.19, bf16[1,3584,1024]{2,1,0:T(8,128)(2,1)} %param.16), kind=kOutput, calls=%fused_computation.25 | convolution fusion | flops 1879048192 | bytes 10223616 | tf_op jit(solution)/shard_map/dot_general | solution.py:207
  338.9 11.8 %fusion.31 = f32[256,3584]{1,0:T(8,128)} fusion(bf16[1,1024,3584]{2,1,0:T(8,128)(2,1)} %param.17, f32[256]{0:T(256)S(1)} %mul.231, f32[256,1024]{1,0:T(8,128)} %fusion.21, bf16[256,3584]{1,0:T(8,128)(2,1)} %copy-done.21, bf16[1,3584,1024]{2,1,0:T(8,128)(2,1)} %param.15), kind=kOutput, calls=%fused_computation.35 | convolution fusion | flops 3760586752 | bytes 21234688 | tf_op jit(solution)/shard_map/dot_general | solution.py:209
  362.4 11.5 %fusion.34 = f32[256,3584]{1,0:T(8,128)} fusion(bf16[1,1024,3584]{2,1,0:T(8,128)(2,1)} %param.17, f32[256]{0:T(256)S(1)} %mul.241, f32[256,1024]{1,0:T(8,128)S(1)} %fusion.19, bf16[256,3584]{1,0:T(8,128)(2,1)} %copy-done.16, bf16[1,3584,1024]{2,1,0:T(8,128)(2,1)} %param.15), kind=kOutput, calls=%fused_computation.36 | convolution fusion | flops 3760586752 | bytes 21234688 | tf_op jit(solution)/shard_map/dot_general | solution.py:209
  382.7 6.1 %fusion.17 = f32[256,1024]{1,0:T(8,128)} fusion(bf16[256,3584]{1,0:T(8,128)(2,1)S(1)} %constant_dynamic-update-slice_fusion.25, bf16[1,3584,1024]{2,1,0:T(8,128)(2,1)} %param.16), kind=kOutput, calls=%fused_computation.21 | convolution fusion | flops 1879048192 | bytes 10223616 | tf_op jit(solution)/shard_map/dot_general | solution.py:207
  388.8 11.9 %fusion.37 = f32[256,3584]{1,0:T(8,128)} fusion(bf16[1,1024,3584]{2,1,0:T(8,128)(2,1)} %param.17, f32[256]{0:T(256)S(1)} %mul.246, f32[256,1024]{1,0:T(8,128)} %fusion.17, bf16[256,3584]{1,0:T(8,128)(2,1)} %copy-done.18, bf16[1,3584,1024]{2,1,0:T(8,128)(2,1)} %param.15), kind=kOutput, calls=%fused_computation.37 | convolution fusion | flops 3760586752 | bytes 21234688 | tf_op jit(solution)/shard_map/dot_general | solution.py:209
  408.2 10.2 %collective-permute-done.21 = bf16[64,3584]{1,0:T(8,128)(2,1)S(1)} collective-permute-done((bf16[64,3584]{1,0:T(8,128)(2,1)S(1)}, bf16[64,3584]{1,0:T(8,128)(2,1)S(1)}, u32[]{:S(2)}, u32[]{:S(2)}) %collective-permute-start.21) | collective-permute-done | bytes 458784 | tf_op jit(solution)/shard_map/ppermute | solution.py:109
  421.5 7.5 %collective-permute-done.32 = bf16[64,3584]{1,0:T(8,128)(2,1)S(1)} collective-permute-done((bf16[64,3584]{1,0:T(8,128)(2,1)S(1)}, bf16[64,3584]{1,0:T(8,128)(2,1)S(1)}, u32[]{:S(2)}, u32[]{:S(2)}) %collective-permute-start.32) | collective-permute-done | bytes 458784 | tf_op jit(solution)/shard_map/ppermute | solution.py:113
  438.3 6.8 %collective-permute-done.33 = bf16[64,3584]{1,0:T(8,128)(2,1)S(1)} collective-permute-done((bf16[64,3584]{1,0:T(8,128)(2,1)S(1)}, bf16[64,3584]{1,0:T(8,128)(2,1)S(1)}, u32[]{:S(2)}, u32[]{:S(2)}) %collective-permute-start.33) | collective-permute-done | bytes 458784 | tf_op jit(solution)/shard_map/ppermute | solution.py:109
  (212 shorter events, 140.2 us)
Async XLA Ops:
  0.0 47.1 %collective-permute-start = (bf16[64,16,128]{2,1,0:T(8,128)(2,1)}, bf16[64,16,128]{2,1,0:T(8,128)(2,1)}, u32[]{:S(2)}, u32[]{:S(2)}) collective-permute-start(bf16[64,16,128]{2,1,0:T(8,128)(2,1)} %param.12), channel_id=1, source_target_pairs={{0,2},{2,0},{1,3},{3,1},{4,6},{6,4},{5,7},{7,5},{8,10},{10,8},{9,1... | collective-permute-start | bytes 786440 | tf_op jit(solution)/shard_map/ppermute | solution.py:113
  3.0 33.5 %collective-permute-start.1 = (bf16[64,16,128]{2,1,0:T(8,128)(2,1)}, bf16[64,16,128]{2,1,0:T(8,128)(2,1)}, u32[]{:S(2)}, u32[]{:S(2)}) collective-permute-start(bf16[64,16,128]{2,1,0:T(8,128)(2,1)} %param.12), channel_id=1, source_target_pairs={{0,4},{4,8},{8,12},{12,0},{1,5},{5,9},{9,13},{13,1},{2,6},{6,10},{... | collective-permute-start | bytes 786440 | tf_op jit(solution)/shard_map/ppermute | solution.py:109
  4.5 105.4 %collective-permute-start.8 = (bf16[8192,224]{0,1:T(8,128)(2,1)}, bf16[8192,224]{0,1:T(8,128)(2,1)}, u32[]{:S(2)}, u32[]{:S(2)}) collective-permute-start(bf16[8192,224]{0,1:T(8,128)(2,1)} %param.13), channel_id=1, source_target_pairs={{0,1},{1,0},{2,3},{3,2},{4,5},{5,4},{6,7},{7,6},{8,9},{9,8},{10,11... | collective-permute-start | bytes 11010056 | tf_op jit(solution)/shard_map/ppermute | solution.py:117
  66.4 26.5 %collective-permute-start.7 = (bf16[64,128,128]{2,1,0:T(8,128)(2,1)}, bf16[64,128,128]{2,1,0:T(8,128)(2,1)S(1)}, u32[]{:S(2)}, u32[]{:S(2)}) collective-permute-start(bf16[64,128,128]{2,1,0:T(8,128)(2,1)} %get-tuple-element.18), channel_id=1, source_target_pairs={{0,1},{1,0},{2,3},{3,2},{4,5},{5,4},{6,7},{7,6},{8,9},{9,8},{10,11... | collective-permute-start | bytes 6291464 | tf_op jit(solution)/shard_map/ppermute | solution.py:117
  109.4 29.3 %collective-permute-start.9 = (bf16[64,8192]{1,0:T(8,128)(2,1)S(1)}, bf16[64,8192]{1,0:T(8,128)(2,1)S(1)}, u32[]{:S(2)}, u32[]{:S(2)}) collective-permute-start(bf16[64,8192]{1,0:T(8,128)(2,1)S(1)} %bitcast.160), channel_id=1, source_target_pairs={{0,2},{2,0},{1,3},{3,1},{4,6},{6,4},{5,7},{7,5},{8,10},{10,8},{9,1... | collective-permute-start | bytes 3145736 | tf_op jit(solution)/shard_map/ppermute | solution.py:113
  109.8 27.3 %collective-permute-start.10 = (bf16[64,8192]{1,0:T(8,128)(2,1)S(1)}, bf16[64,8192]{1,0:T(8,128)(2,1)S(1)}, u32[]{:S(2)}, u32[]{:S(2)}) collective-permute-start(bf16[64,8192]{1,0:T(8,128)(2,1)S(1)} %bitcast.161), channel_id=1, source_target_pairs={{0,4},{4,8},{8,12},{12,0},{1,5},{5,9},{9,13},{13,1},{2,6},{6,10},{... | collective-permute-start | bytes 3145736 | tf_op jit(solution)/shard_map/ppermute | solution.py:109
  137.1 28.1 %collective-permute-start.11 = (bf16[64,8192]{1,0:T(8,128)(2,1)S(1)}, bf16[64,8192]{1,0:T(8,128)(2,1)S(1)}, u32[]{:S(2)}, u32[]{:S(2)}) collective-permute-start(bf16[64,8192]{1,0:T(8,128)(2,1)S(1)} %collective-permute-done.10), channel_id=1, source_target_pairs={{0,2},{2,0},{1,3},{3,1},{4,6},{6,4},{5,7},{7,5},{8,10},{10,8},{9,1... | collective-permute-start | bytes 3145736 | tf_op jit(solution)/shard_map/ppermute | solution.py:113
  138.8 26.0 %collective-permute-start.12 = (bf16[64,8192]{1,0:T(8,128)(2,1)S(1)}, bf16[64,8192]{1,0:T(8,128)(2,1)S(1)}, u32[]{:S(2)}, u32[]{:S(2)}) collective-permute-start(bf16[64,8192]{1,0:T(8,128)(2,1)S(1)} %collective-permute-done.10), channel_id=1, source_target_pairs={{0,4},{4,8},{8,12},{12,0},{1,5},{5,9},{9,13},{13,1},{2,6},{6,10},{... | collective-permute-start | bytes 3145736 | tf_op jit(solution)/shard_map/ppermute | solution.py:109
  164.8 26.8 %collective-permute-start.13 = (bf16[64,8192]{1,0:T(8,128)(2,1)S(1)}, bf16[64,8192]{1,0:T(8,128)(2,1)S(1)}, u32[]{:S(2)}, u32[]{:S(2)}) collective-permute-start(bf16[64,8192]{1,0:T(8,128)(2,1)S(1)} %collective-permute-done.12), channel_id=1, source_target_pairs={{0,2},{2,0},{1,3},{3,1},{4,6},{6,4},{5,7},{7,5},{8,10},{10,8},{9,1... | collective-permute-start | bytes 3145736 | tf_op jit(solution)/shard_map/ppermute | solution.py:113
  165.2 24.9 %collective-permute-start.14 = (bf16[64,8192]{1,0:T(8,128)(2,1)S(1)}, bf16[64,8192]{1,0:T(8,128)(2,1)S(1)}, u32[]{:S(2)}, u32[]{:S(2)}) collective-permute-start(bf16[64,8192]{1,0:T(8,128)(2,1)S(1)} %collective-permute-done.12), channel_id=1, source_target_pairs={{0,4},{4,8},{8,12},{12,0},{1,5},{5,9},{9,13},{13,1},{2,6},{6,10},{... | collective-permute-start | bytes 3145736 | tf_op jit(solution)/shard_map/ppermute | solution.py:109
  190.1 22.2 %collective-permute-start.15 = (bf16[64,8192]{1,0:T(8,128)(2,1)S(1)}, bf16[64,8192]{1,0:T(8,128)(2,1)S(1)}, u32[]{:S(2)}, u32[]{:S(2)}) collective-permute-start(bf16[64,8192]{1,0:T(8,128)(2,1)S(1)} %collective-permute-done.14), channel_id=1, source_target_pairs={{0,2},{2,0},{1,3},{3,1},{4,6},{6,4},{5,7},{7,5},{8,10},{10,8},{9,1... | collective-permute-start | bytes 3145736 | tf_op jit(solution)/shard_map/ppermute | solution.py:113
  239.6 24.9 %collective-permute-start.34 = (bf16[64,3584]{1,0:T(8,128)(2,1)S(1)}, bf16[64,3584]{1,0:T(8,128)(2,1)S(1)}, u32[]{:S(2)}, u32[]{:S(2)}) collective-permute-start(bf16[64,3584]{1,0:T(8,128)(2,1)S(1)} %multiply_convert_fusion.4), channel_id=1, source_target_pairs={{0,2},{2,0},{1,3},{3,1},{4,6},{6,4},{5,7},{7,5},{8,10},{10,8},{9,1... | collective-permute-start | bytes 1376264 | tf_op jit(solution)/shard_map/ppermute | solution.py:113
  264.5 41.4 %collective-permute-start.35 = (bf16[128,3584]{1,0:T(8,128)(2,1)S(1)}, bf16[128,3584]{1,0:T(8,128)(2,1)S(1)}, u32[]{:S(2)}, u32[]{:S(2)}) collective-permute-start(bf16[128,3584]{1,0:T(8,128)(2,1)S(1)} %pad_maximum_fusion.4), channel_id=1, source_target_pairs={{0,1},{1,0},{2,3},{3,2},{4,5},{5,4},{6,7},{7,6},{8,9},{9,8},{10,11... | collective-permute-start | bytes 2752520 | tf_op jit(solution)/shard_map/ppermute | solution.py:117
  292.0 38.3 %collective-permute-start.18 = (bf16[128,3584]{1,0:T(8,128)(2,1)}, bf16[128,3584]{1,0:T(8,128)(2,1)}, u32[]{:S(2)}, u32[]{:S(2)}) collective-permute-start(bf16[128,3584]{1,0:T(8,128)(2,1)} %pad_maximum_fusion.1), channel_id=1, source_target_pairs={{0,1},{1,0},{2,3},{3,2},{4,5},{5,4},{6,7},{7,6},{8,9},{9,8},{10,11... | collective-permute-start | bytes 2752520 | tf_op jit(solution)/shard_map/ppermute | solution.py:117
  295.3 32.9 %collective-permute-start.28 = (bf16[64,3584]{1,0:T(8,128)(2,1)S(1)}, bf16[64,3584]{1,0:T(8,128)(2,1)S(1)}, u32[]{:S(2)}, u32[]{:S(2)}) collective-permute-start(bf16[64,3584]{1,0:T(8,128)(2,1)S(1)} %collective-permute-done.22), channel_id=1, source_target_pairs={{0,4},{4,8},{8,12},{12,0},{1,5},{5,9},{9,13},{13,1},{2,6},{6,10},{... | collective-permute-start | bytes 1376264 | tf_op jit(solution)/shard_map/ppermute | solution.py:109
  305.9 49.9 %collective-permute-start.24 = (bf16[128,3584]{1,0:T(8,128)(2,1)}, bf16[128,3584]{1,0:T(8,128)(2,1)S(1)}, u32[]{:S(2)}, u32[]{:S(2)}) collective-permute-start(bf16[128,3584]{1,0:T(8,128)(2,1)} %pad_maximum_fusion.2), channel_id=1, source_target_pairs={{0,1},{1,0},{2,3},{3,2},{4,5},{5,4},{6,7},{7,6},{8,9},{9,8},{10,11... | collective-permute-start | bytes 2752520 | tf_op jit(solution)/shard_map/ppermute | solution.py:117
  327.8 91.7 %collective-permute-start.36 = (bf16[128,3584]{1,0:T(8,128)(2,1)}, bf16[128,3584]{1,0:T(8,128)(2,1)}, u32[]{:S(2)}, u32[]{:S(2)}) collective-permute-start(bf16[128,3584]{1,0:T(8,128)(2,1)} %slice.162), channel_id=1, source_target_pairs={{0,1},{1,0},{2,3},{3,2},{4,5},{5,4},{6,7},{7,6},{8,9},{9,8},{10,11... | collective-permute-start | bytes 2752520 | tf_op jit(solution)/shard_map/ppermute | solution.py:117
  328.3 25.1 %collective-permute-start.29 = (bf16[64,3584]{1,0:T(8,128)(2,1)S(1)}, bf16[64,3584]{1,0:T(8,128)(2,1)S(1)}, u32[]{:S(2)}, u32[]{:S(2)}) collective-permute-start(bf16[64,3584]{1,0:T(8,128)(2,1)S(1)} %collective-permute-done.28), channel_id=1, source_target_pairs={{0,2},{2,0},{1,3},{3,1},{4,6},{6,4},{5,7},{7,5},{8,10},{10,8},{9,1... | collective-permute-start | bytes 1376264 | tf_op jit(solution)/shard_map/ppermute | solution.py:113
  353.4 22.3 %collective-permute-start.19 = (bf16[128,3584]{1,0:T(8,128)(2,1)}, bf16[128,3584]{1,0:T(8,128)(2,1)}, u32[]{:S(2)}, u32[]{:S(2)}) collective-permute-start(bf16[128,3584]{1,0:T(8,128)(2,1)} %slice.165), channel_id=1, source_target_pairs={{0,1},{1,0},{2,3},{3,2},{4,5},{5,4},{6,7},{7,6},{8,9},{9,8},{10,11... | collective-permute-start | bytes 2752520 | tf_op jit(solution)/shard_map/ppermute | solution.py:117
  354.4 25.6 %collective-permute-start.30 = (bf16[128,3584]{1,0:T(8,128)(2,1)}, bf16[128,3584]{1,0:T(8,128)(2,1)}, u32[]{:S(2)}, u32[]{:S(2)}) collective-permute-start(bf16[128,3584]{1,0:T(8,128)(2,1)} %pad_maximum_fusion.3), channel_id=1, source_target_pairs={{0,1},{1,0},{2,3},{3,2},{4,5},{5,4},{6,7},{7,6},{8,9},{9,8},{10,11... | collective-permute-start | bytes 2752520 | tf_op jit(solution)/shard_map/ppermute | solution.py:117
  375.6 28.3 %collective-permute-start.25 = (bf16[128,3584]{1,0:T(8,128)(2,1)S(1)}, bf16[128,3584]{1,0:T(8,128)(2,1)}, u32[]{:S(2)}, u32[]{:S(2)}) collective-permute-start(bf16[128,3584]{1,0:T(8,128)(2,1)S(1)} %slice.164), channel_id=1, source_target_pairs={{0,1},{1,0},{2,3},{3,2},{4,5},{5,4},{6,7},{7,6},{8,9},{9,8},{10,11... | collective-permute-start | bytes 2752520 | tf_op jit(solution)/shard_map/ppermute | solution.py:117
  378.4 24.1 %collective-permute-start.20 = (bf16[64,3584]{1,0:T(8,128)(2,1)}, bf16[64,3584]{1,0:T(8,128)(2,1)}, u32[]{:S(2)}, u32[]{:S(2)}) collective-permute-start(bf16[64,3584]{1,0:T(8,128)(2,1)} %slice.169), channel_id=1, source_target_pairs={{0,2},{2,0},{1,3},{3,1},{4,6},{6,4},{5,7},{7,5},{8,10},{10,8},{9,1... | collective-permute-start | bytes 1376264 | tf_op jit(solution)/shard_map/ppermute | solution.py:113
  406.5 22.6 %collective-permute-start.32 = (bf16[64,3584]{1,0:T(8,128)(2,1)S(1)}, bf16[64,3584]{1,0:T(8,128)(2,1)S(1)}, u32[]{:S(2)}, u32[]{:S(2)}) collective-permute-start(bf16[64,3584]{1,0:T(8,128)(2,1)S(1)} %slice.167), channel_id=1, source_target_pairs={{0,2},{2,0},{1,3},{3,1},{4,6},{6,4},{5,7},{7,5},{8,10},{10,8},{9,1... | collective-permute-start | bytes 1376264 | tf_op jit(solution)/shard_map/ppermute | solution.py:113
  421.1 17.2 %collective-permute-start.37 = (bf16[64,3584]{1,0:T(8,128)(2,1)S(1)}, bf16[64,3584]{1,0:T(8,128)(2,1)S(1)}, u32[]{:S(2)}, u32[]{:S(2)}) collective-permute-start(bf16[64,3584]{1,0:T(8,128)(2,1)S(1)} %slice.166), channel_id=1, source_target_pairs={{0,2},{2,0},{1,3},{3,1},{4,6},{6,4},{5,7},{7,5},{8,10},{10,8},{9,1... | collective-permute-start | bytes 1376264 | tf_op jit(solution)/shard_map/ppermute | solution.py:113
  (44 other events, 587.2 us)

commit v2 on v1

--- a/solution.py
+++ b/solution.py
@@ -1,6 +1,8 @@
 import jax
 import jax.numpy as jnp
 from jax import lax
+from jax.experimental import pallas as pl
+from jax.experimental.pallas import tpu as pltpu
 from jax.sharding import Mesh, PartitionSpec as P
 
 LAT = 256
@@ -105,6 +107,11 @@
     return (attn32 + mixed).astype(jnp.bfloat16)
 
 
+CHIPS = [(r, b) for r in range(NZ) for b in range(NY)]
+NT = (((1,), (1,)), ((), ()))
+F32, B16 = jnp.float32, jnp.bfloat16
+
+
 def shift_z(value):
     return lax.ppermute(value, "z", [(i, (i + 1) % NZ) for i in range(NZ)])
 
@@ -117,13 +124,204 @@
     return lax.ppermute(value, "core", [(0, 1), (1, 0)])
 
 
+def hand_back(value, r, b):
+    if r == 0 and b == 0:
+        return value
+    pairs = [
+        (z * NY + y, ((z - r) % NZ) * NY + (y ^ b)) for z in range(NZ) for y in range(NY)
+    ]
+    return lax.ppermute(value, ("z", "y"), pairs)
+
+
 def ring(block):
-    pieces = []
+    pieces = {}
     for r in range(NZ):
-        pieces.append((block, swap_y(block)))
+        pieces[r, 0] = block
+        pieces[r, 1] = swap_y(block)
         if r < NZ - 1:
             block = shift_z(block)
     return pieces
+
+
+def whole_block(shape):
+    return pl.BlockSpec(shape, lambda i, *_: (0,) * len(shape))
+
+
+def attend(q_own, q_other, k_own, k_other, query_place, key_place):
+    heads, tok, width = q_own.shape
+    half, wide = k_own.shape
+    rows = 2 * tok
+    hb = 2
+    turn = score_scale * 1.4426950408889634
+
+    def kernel(qp, kp, qo, qx, ko, kx, out, bias):
+        @pl.when(pl.program_id(0) == 0)
+        def _():
+            for j in range(hb):
+                bias[j * rows : (j + 1) * rows] = jnp.where(qp[...] >= kp[...], 0.0, -1e30)
+
+        q = jnp.concatenate([ref[j] for j in range(hb) for ref in (qo, qx)], axis=0)
+        s0 = lax.dot_general(q, ko[:, :width], NT, preferred_element_type=F32) + bias[:, :half]
+        s1 = lax.dot_general(q, kx[:, :width], NT, preferred_element_type=F32) + bias[:, half:]
+        top = jnp.maximum(
+            jnp.max(s0, axis=-1, keepdims=True), jnp.max(s1, axis=-1, keepdims=True)
+        )
+        p0 = jnp.exp2((s0 - top) * turn)
+        p1 = jnp.exp2((s1 - top) * turn)
+        total = jnp.sum(p0, axis=-1, keepdims=True) + jnp.sum(p1, axis=-1, keepdims=True)
+        acc = jnp.dot(p0.astype(B16), ko[:, :LAT], preferred_element_type=F32)
+        acc = acc + jnp.dot(p1.astype(B16), kx[:, :LAT], preferred_element_type=F32)
+        latent = (acc / total).astype(B16)
+        for j in range(hb):
+            out[j] = latent[j * rows : (j + 1) * rows]
+
+    return pl.pallas_call(
+        kernel,
+        grid=(heads // hb,),
+        in_specs=[
+            whole_block((rows, 1)),
+            whole_block((1, 2 * half)),
+            pl.BlockSpec((hb, tok, width), lambda i: (i, 0, 0)),
+            pl.BlockSpec((hb, tok, width), lambda i: (i, 0, 0)),
+            whole_block((half, wide)),
+            whole_block((half, wide)),
+        ],
+        out_specs=pl.BlockSpec((hb, rows, LAT), lambda i: (i, 0, 0)),
+        out_shape=jax.ShapeDtypeStruct((heads, rows, LAT), B16),
+        scratch_shapes=[pltpu.VMEM((hb * rows, 2 * half), F32)],
+        compiler_params=pltpu.CompilerParams(vmem_limit_bytes=32 << 20),
+        cost_estimate=pl.CostEstimate(
+            flops=2 * heads * rows * 2 * half * (width + LAT),
+            bytes_accessed=8 << 20,
+            transcendentals=heads * rows * 2 * half,
+        ),
+        name="attend",
+    )(query_place, key_place, q_own, q_other, k_own, k_other)
+
+
+def raise_values(latent, pieces, at):
+    heads, rows, _ = latent.shape
+    hb = 8
+    part = pieces[0, 0].shape[1]
+
+    def kernel(where, lat, *refs):
+        parts, out, lift = refs[: len(CHIPS)], refs[-2], refs[-1]
+        for n, ref in enumerate(parts):
+            lift[:, pl.ds(pl.multiple_of(where[n] * part, part), part), :] = ref[...]
+        for j in range(hb):
+            out[:, j * VD : (j + 1) * VD] = jnp.dot(
+                lat[j], lift[j], preferred_element_type=F32
+            ).astype(B16)
+
+    return pl.pallas_call(
+        kernel,
+        grid_spec=pltpu.PrefetchScalarGridSpec(
+            num_scalar_prefetch=1,
+            grid=(heads // hb,),
+            in_specs=[pl.BlockSpec((hb, rows, LAT), lambda i, _: (i, 0, 0))]
+            + [pl.BlockSpec((hb, part, VD), lambda i, _: (i, 0, 0))] * len(CHIPS),
+            out_specs=pl.BlockSpec((rows, hb * VD), lambda i, _: (0, i)),
+            scratch_shapes=[pltpu.VMEM((hb, LAT, VD), B16)],
+        ),
+        out_shape=jax.ShapeDtypeStruct((rows, heads * VD), B16),
+        compiler_params=pltpu.CompilerParams(vmem_limit_bytes=24 << 20),
+        cost_estimate=pl.CostEstimate(
+            flops=2 * heads * rows * LAT * VD, bytes_accessed=6 << 20, transcendentals=0
+        ),
+        name="raise_values",
+    )(at, latent, *[pieces[chip] for chip in CHIPS])
+
+
+def normalise(strips, at, norm_gain):
+    tok, cols = strips[0, 0].shape
+    wide = NY * cols
+
+    def kernel(where, gain, *refs):
+        parts, attn, normed, pair, square = refs[: len(CHIPS)], *refs[-4:]
+        square[...] = jnp.zeros_like(square)
+        for r in range(NZ):
+            low, high = parts[NY * r][...].astype(F32), parts[NY * r + 1][...].astype(F32)
+            swap = jnp.full((tok, cols), where[0], jnp.int32) == 1
+            pair[:, :cols] = jnp.where(swap, high, low)
+            pair[:, cols:] = jnp.where(swap, low, high)
+            both = pair[...]
+            attn[:, pl.ds(pl.multiple_of(where[1 + r] * wide, 128), wide)] = both.astype(B16)
+            square[...] += jnp.sum(both * both, axis=-1, keepdims=True)
+        scale = lax.rsqrt(square[...] / (NZ * wide) + 1e-06)
+        normed[...] = (attn[...].astype(F32) * scale * gain[...]).astype(B16)
+
+    shape = jax.ShapeDtypeStruct((tok, NZ * wide), B16)
+    return pl.pallas_call(
+        kernel,
+        grid_spec=pltpu.PrefetchScalarGridSpec(
+            num_scalar_prefetch=1,
+            grid=(1,),
+            in_specs=[whole_block((1, NZ * wide))] + [whole_block((tok, cols))] * len(CHIPS),
+            out_specs=[whole_block((tok, NZ * wide))] * 2,
+            scratch_shapes=[pltpu.VMEM((tok, wide), F32), pltpu.VMEM((tok, 1), F32)],
+        ),
+        out_shape=[shape, shape],
+        compiler_params=pltpu.CompilerParams(vmem_limit_bytes=16 << 20),
+        cost_estimate=pl.CostEstimate(flops=1 << 20, bytes_accessed=2 << 20, transcendentals=0),
+        name="normalise",
+    )(at, norm_gain.reshape(1, -1), *[strips[chip] for chip in CHIPS])
+
+
+def expert(blocks, shares, gate_proj, up_proj, down_proj):
+    tok, width = blocks[0].shape
+    hidden_units = gate_proj.shape[2]
+    fb = 256
+    n = len(blocks)
+    rows = n * tok
+    steps = hidden_units // fb
+
+    def kernel(share, gate_w, up_w, down_w, *refs):
+        ins, outs, x, acc = refs[:n], refs[n : 2 * n], refs[-2], refs[-1]
+        step = pl.program_id(0)
+
+        @pl.when(step == 0)
+        def _():
+            for j in range(n):
+                x[j * tok : (j + 1) * tok] = ins[j][...]
+
+        gate = jnp.dot(x[...], gate_w[0], preferred_element_type=F32)
+        upper = jnp.dot(x[...], up_w[0], preferred_element_type=F32)
+        hidden = (jax.nn.silu(gate) * upper).astype(B16)
+        down = jnp.dot(hidden, down_w[0], preferred_element_type=F32)
+
+        @pl.when(step == 0)
+        def _():
+            acc[...] = down
+
+        @pl.when((step > 0) & (step < steps - 1))
+        def _():
+            acc[...] += down
+
+        @pl.when(step == steps - 1)
+        def _():
+            out = ((acc[...] + down) * share[...]).astype(B16)
+            for j in range(n):
+                outs[j][...] = out[j * tok : (j + 1) * tok]
+
+    return pl.pallas_call(
+        kernel,
+        grid=(steps,),
+        in_specs=[
+            whole_block((rows, 1)),
+            pl.BlockSpec((1, width, fb), lambda i: (0, 0, i)),
+            pl.BlockSpec((1, width, fb), lambda i: (0, 0, i)),
+            pl.BlockSpec((1, fb, width), lambda i: (0, i, 0)),
+        ]
+        + [whole_block((tok, width))] * n,
+        out_specs=[whole_block((tok, width))] * n,
+        out_shape=[jax.ShapeDtypeStruct((tok, width), B16)] * n,
+        scratch_shapes=[pltpu.VMEM((rows, width), B16), pltpu.VMEM((rows, width), F32)],
+        compiler_params=pltpu.CompilerParams(vmem_limit_bytes=40 << 20),
+        cost_estimate=pl.CostEstimate(
+            flops=6 * rows * width * hidden_units, bytes_accessed=26 << 20, transcendentals=0
+        ),
+        name="expert",
+    )(shares, gate_proj, up_proj, down_proj, *blocks)
 
 
 def boxed(
@@ -138,15 +336,12 @@
     routes,
     route_weights,
 ):
-    f32, b16 = jnp.float32, jnp.bfloat16
     tok, heads, width = queries.shape
     z, y, core = (lax.axis_index(name) for name in ("z", "y", "core"))
+    experts = NZ * NY * NC
     place = (z * NY + y) * NC + core
-    experts = NZ * NY * NC
-    whole = ("z", "y", "core")
-
-    def origin(d, r, b):
-        return (((z - r) % NZ) * NY + (y ^ b)) * NC + (core ^ d)
+    first = core == 0
+    hh = heads // NC
 
     dense = jnp.sum(
         jnp.where(
@@ -154,76 +349,80 @@
         ),
         axis=1,
     )
-    keys = lax.all_gather(kv_latent, whole, axis=0, tiled=True)
-    dense_all = lax.all_gather(dense, whole, axis=0, tiled=True)
-
-    lift_rows = jnp.concatenate([p for pair in ring(value_up) for p in pair], axis=1)
-    lift = jnp.concatenate([lift_rows, swap_core(lift_rows)], axis=1)
-    part = value_up.shape[1]
-    order = jnp.stack([origin(d, r, b) for d in range(NC) for r in range(NZ) for b in range(NY)])
-    lat_order = (order[:, None] * part + jnp.arange(part)[None, :]).reshape(-1)
-    turn = (jnp.arange(LAT)[:, None] == lat_order[None, :]).astype(b16)
-    values = jnp.dot(keys[:, :LAT], turn, preferred_element_type=f32).astype(b16)
-    columns = jnp.concatenate([out_proj, swap_core(out_proj)], axis=1)
-
-    query_place = place * tok + jnp.arange(tok)
-    scores = jnp.einsum("shc,tc->sht", queries, keys, preferred_element_type=f32) * score_scale
-    allowed = (query_place[:, None] >= jnp.arange(keys.shape[0])[None, :])[:, None, :]
-    scores = jnp.where(allowed, scores, -1e30)
-    top = jnp.max(scores, axis=-1)
-    expo = jnp.where(allowed, jnp.exp(scores - top[..., None]), 0.0)
-    total = jnp.sum(expo, axis=-1)
-    acc = jnp.einsum("sht,tc->shc", expo.astype(b16), values, preferred_element_type=f32)
-    latent_out = (acc / total[..., None]).astype(b16)
-    lifted = jnp.einsum("shc,hcv->shv", latent_out, lift, preferred_element_type=f32)
-    flat_heads = lifted.astype(b16).reshape(tok, heads * VD)
-
-    strips = [
-        [jnp.dot(p, columns, preferred_element_type=f32).astype(b16) for p in pair]
-        for pair in ring(flat_heads)
-    ]
-    strips = jnp.stack([s for pair in strips for s in pair])
-    chips = NZ * NY
-    ids = jnp.arange(chips)
-    here = ((z - ids // NY) % NZ) * NY + (y ^ (ids % NY))
-    sent = jnp.take(strips, here, axis=0)
-    got = lax.all_to_all(sent, ("z", "y"), split_axis=0, concat_axis=0, tiled=True)
-    cols = out_proj.shape[1]
-    got = got.reshape(chips, tok, NC, cols)
-    got = jnp.where(core == 0, got, got[:, :, ::-1])
-    attn32 = jnp.transpose(got, (1, 0, 2, 3)).reshape(tok, -1).astype(f32)
-    scale = lax.rsqrt(jnp.mean(attn32 * attn32, axis=-1, keepdims=True) + 1e-06)
-    normed = (attn32 * scale * norm_gain).astype(b16)
-
-    width_d = normed.shape[1]
-    mine = jnp.take(dense_all, place, axis=1).reshape(experts, tok)
-    by_chunk = jnp.stack(
-        [origin(d, r, b) for r in range(NZ) for d in range(NC) for b in range(NY)]
-    )
-    shares = jnp.take(mine, by_chunk, axis=0).reshape(NZ, NC * NY * tok, 1)
-
-    def expert(block, share):
-        gate = jnp.dot(block, gate_proj[0], preferred_element_type=f32)
-        upper = jnp.dot(block, up_proj[0], preferred_element_type=f32)
-        hidden = (jax.nn.silu(gate) * upper).astype(b16)
-        return share * jnp.dot(hidden, down_proj[0], preferred_element_type=f32)
-
-    sums = []
-    for r, pair in enumerate(ring(normed)):
-        own = jnp.concatenate(pair, axis=0)
-        block = jnp.concatenate([own, swap_core(own)], axis=0)
-        out = expert(block, shares[r])
-        half = NY * tok
-        out = out[:half] + swap_core(out[half:].astype(b16)).astype(f32)
-        sums.append(out[:tok] + swap_y(out[tok:].astype(b16)).astype(f32))
+    high = dense.astype(B16)
+    low = (dense - high.astype(F32)).astype(B16)
+    pack = jnp.concatenate([kv_latent, high, low], axis=1)
+    pack = jnp.broadcast_to(pack[None], (len(CHIPS),) + pack.shape)
+    k_own = lax.all_to_all(pack, ("z", "y"), split_axis=0, concat_axis=0, tiled=True)
+    k_own = k_own.reshape(-1, k_own.shape[-1])
+    k_other = swap_core(k_own)
+
+    by_head = jnp.transpose(queries, (1, 0, 2)).reshape(NC, hh, tok, width)
+    q_own = lax.dynamic_index_in_dim(by_head, core, 0, keepdims=False)
+    q_other = swap_core(lax.dynamic_index_in_dim(by_head, 1 - core, 0, keepdims=False))
+    lift = value_up.reshape(NC, hh, -1, VD)
+    lift_own = lax.dynamic_index_in_dim(lift, core, 0, keepdims=False)
+    lift_other = swap_core(lax.dynamic_index_in_dim(lift, 1 - core, 0, keepdims=False))
+    lift = jnp.concatenate(
+        [jnp.where(first, lift_own, lift_other), jnp.where(first, lift_other, lift_own)], axis=1
+    )
+    lift_pieces = ring(lift)
+
+    kk = out_proj.shape[0] // NC
+    proj_own = lax.dynamic_slice_in_dim(out_proj, core * kk, kk, 0)
+    proj_other = swap_core(lax.dynamic_slice_in_dim(out_proj, (1 - core) * kk, kk, 0))
+    columns = jnp.concatenate(
+        [jnp.where(first, proj_own, proj_other), jnp.where(first, proj_other, proj_own)], axis=1
+    )
+
+    steps = jnp.arange(tok)
+    query_place = jnp.concatenate([place * tok + steps, (place ^ 1) * tok + steps])[:, None]
+    chip_rows = jnp.arange(NZ * NY)[:, None] * (NC * tok) + steps[None, :]
+    key_place = jnp.concatenate(
+        [(chip_rows + core * tok).reshape(-1), (chip_rows + (1 - core) * tok).reshape(-1)]
+    )[None, :]
+    latent = attend(q_own, q_other, k_own, k_other, query_place, key_place)
+    down_chips = jnp.stack([((z - r) % NZ) * NY + (y ^ b) for r, b in CHIPS])
+    flat_heads = raise_values(latent, lift_pieces, down_chips)
+
+    strips = {}
+    for chip, piece in ring(flat_heads).items():
+        part = jnp.dot(piece, columns, preferred_element_type=F32)
+        strip = (part[:tok] + swap_core(part[tok:].astype(B16)).astype(F32)).astype(B16)
+        strips[chip] = hand_back(strip, *chip)
+    at = jnp.stack([y] + [(z + r) % NZ for r in range(NZ)])
+    attn, normed = normalise(strips, at, norm_gain)
+
+    def mine(pack):
+        flat = pack[:, width:].astype(F32).reshape(len(CHIPS), tok, 2, experts).sum(axis=2)
+        return jnp.take(flat, place, axis=2)
+
+    shares = [mine(k_own), mine(k_other)]
+
+    sums = {}
+    pieces = ring(normed)
+    for r in range(NZ):
+        blocks = [pieces[r, b] for b in range(NY)]
+        blocks += [swap_core(block) for block in blocks]
+        share = jnp.concatenate(
+            [
+                lax.dynamic_index_in_dim(shares[d], ((z - r) % NZ) * NY + (y ^ b), 0, False)
+                for d in range(NC)
+                for b in range(NY)
+            ]
+        )[:, None]
+        out = expert(blocks, share, gate_proj, up_proj, down_proj)
+        far = out[1].astype(F32) + swap_core(out[3]).astype(F32)
+        near = out[0].astype(F32) + swap_core(out[2]).astype(F32)
+        sums[r] = near + swap_y(far.astype(B16)).astype(F32)
     acc = sums[1]
     for r in (2, 3, 0):
-        acc = shift_z(acc.astype(b16)).astype(f32) + sums[r]
-    return (attn32 + acc).astype(b16)
+        acc = shift_z(acc.astype(B16)).astype(F32) + sums[r]
+    return (attn.astype(F32) + acc).astype(B16)
 
 
 def solution(mesh):
-    names = "expert"
+    names = ("expert",)
     body = local
     if mesh.shape["expert"] == NZ * NY * NC and mesh.shape["tensor"] == 1:
         groups = mesh.shape["groups"]
@@ -232,7 +431,7 @@
         )
         names = ("z", "y", "core")
         body = boxed
-    every = ("groups",) + (names if isinstance(names, tuple) else (names,))
+    every = ("groups",) + names
     in_specs = (
         P(every, "tensor", None),
         P(every, None),

time: 453 us -> 320 us (0.71); the launches traced: 446 us -> 319 us
  matrix products: 120 us -> 23.9 us
  Pallas kernels: 0 us -> 64.2 us
  blocking collectives: 45.9 us -> 0 us
  waiting for transfers between devices: 171 us -> 146 us
  starting transfers between devices: 22.5 us -> 47.2 us
  local copies, waits for them, and re-layouts: 50.3 us -> 25.9 us
  other arithmetic: 34.8 us -> 11.1 us
    dot_general x19 -> x8, matrix products: 120 us -> 23.9 us  [boxed(): part = jnp.dot(piece, columns, preferred_element_type=F32)]
    pallas_call x0 -> x7, Pallas kernels: none -> 64.2 us  [the longest x4 44.5 us: expert(): pl.pallas_call(kernel, grid=(steps,), in_specs=[whole_block((rows, 1)), p...]
    all_gather x2 -> x0, blocking collectives: 45.9 us -> none  [the longest x1 23.8 us: boxed(): keys = lax.all_gather(kv_latent, whole, axis=0, tiled=True)]
    ppermute x16, waiting for transfers between devices: 54.3 us -> 31.3 us  [swap_y(): return lax.ppermute(value, 'y', [(0, 1), (1, 0)])]
    sub x1 -> x0, other arithmetic: 20.3 us -> none  [boxed(): expo = jnp.where(allowed, jnp.exp(scores - top[..., None]), 0.0)]
    ppermute x12, waiting for transfers between devices: 106 us -> 90.2 us  [shift_z(): return lax.ppermute(value, 'z', [(i, (i + 1) % NZ) for i in range(NZ)])]
    ppermute x0 -> x7, starting transfers between devices: none -> 14.7 us  [hand_back(): return lax.ppermute(value, ('z', 'y'), pairs)]
    unnamed x73 -> x40, local copies, waits for them, and re-layouts: 24.2 us -> 15.3 us
  transfers between devices with their start and end apart: 39 -> 64, of which waited for: 18 -> 23; matrix products, arithmetic and copies ran while one was open for 41% -> 15% of each run, Pallas kernels for 0% -> 20%
where the time goes in v2:
time: 320 us; the launch traced here: 319 us
  waiting for transfers between devices  146 us (46%)
  Pallas kernels  64.2 us (20%)
  starting transfers between devices  47.2 us (15%)
  local copies, waits for them, and re-layouts  25.9 us (8%)
  matrix products  23.9 us (7%)
  other arithmetic  11.1 us (3%)
    ppermute x12, waiting for transfers between devices, shift_z(): return lax.ppermute(value, 'z', [(i, (i + 1) % NZ) for i in range(NZ)])  90.2 us
    pallas_call x4, Pallas kernels, expert(): pl.pallas_call(kernel, grid=(steps,), in_specs=[whole_block((rows, 1)), p...  44.5 us
    ppermute x16, waiting for transfers between devices, swap_y(): return lax.ppermute(value, 'y', [(0, 1), (1, 0)])  31.3 us
    dot_general x8, matrix products, boxed(): part = jnp.dot(piece, columns, preferred_element_type=F32)  23.9 us
    ppermute x16, starting transfers between devices, swap_y(): return lax.ppermute(value, 'y', [(0, 1), (1, 0)])  17.2 us
    pallas_call x1, Pallas kernels, attend(): pl.pallas_call(kernel, grid=(heads // hb,), in_specs=[whole_block((rows,...  16.6 us
    unnamed x40, local copies, waits for them, and re-layouts  15.3 us
    ppermute x7, starting transfers between devices, hand_back(): return lax.ppermute(value, ('z', 'y'), pairs)  14.7 us
  transfers between devices with their start and end apart: 64, of which 23 were waited for; matrix products, arithmetic and copies ran while one was open for 15% of the time, Pallas kernels for 20%

profile of v2, /device:TPU:0, one launch (start us, length us, event | category | flops | bytes accessed | tf_op | source)
XLA Modules:
  0.0 318.8 jit_solution(795466403504415621)
XLA Ops:
  13.0 4.8 %all-to-all-start = ((bf16[8,64,320]{2,1,0:T(8,128)(2,1)}), bf16[8,64,320]{2,1,0:T(8,128)(2,1)S(1)}, u32[]{:S(2)}, u32[]{:S(2)}) async-start(bf16[8,64,320]{2,1,0:T(8,128)(2,1)} %broadcast_in_dim.54), calls=%async_computation | async-start | bytes 786432 | tf_op jit(solution)/shard_map/all_to_all | solution.py:356
  21.4 14.1 %all-to-all-done = bf16[8,64,320]{2,1,0:T(8,128)(2,1)S(1)} async-done(((bf16[8,64,320]{2,1,0:T(8,128)(2,1)}), bf16[8,64,320]{2,1,0:T(8,128)(2,1)S(1)}, u32[]{:S(2)}, u32[]{:S(2)}) %all-to-all-start) | async-done | bytes 327712 | tf_op jit(solution)/shard_map/all_to_all | solution.py:356
  41.0 5.0 %collective-permute-done.8.refs_6_ = bf16[32,32,128]{2,1,0:T(8,128)(2,1)S(1)} collective-permute-done((bf16[32,32,128]{2,1,0:T(8,128)(2,1)S(1)}, bf16[32,32,128]{2,1,0:T(8,128)(2,1)S(1)}, u32[]{:S(2)}, u32[]{:S(2)}) %collective-permute-start.8) | collective-permute-done | bytes 262176 | tf_op jit(solution)/shard_map/ppermute | solution.py:116
  48.1 16.6 %attend.1.lat = bf16[32,128,256]{2,1,0:T(8,128)(2,1)S(1)} custom-call(s32[128,1]{1,0:T(8,128)S(1)} %copy.90.qp, s32[1,1024]{1,0:T(1,128)S(1)} %bitcast.96, bf16[32,64,288]{2,1,0:T(8,128)(2,1)S(1)} %bitcast.92, bf16[32,64,288]{2,1,0:T(8,128)(2,1)} %collective-permute-done.qx, bf16[512,320]{1,0:T(8,128)(2,1)S(1)} %bitcast.94, ...), custom_call_target="tpu_custom_call" | custom-call | flops 4563402752 | bytes 8388608 | tf_op jit(solution)/shard_map/attend/pallas_call | solution.py:178
  71.7 21.2 %collective-permute-done.15 = bf16[128,4096]{1,0:T(8,128)(2,1)} collective-permute-done((bf16[128,4096]{1,0:T(8,128)(2,1)S(1)}, bf16[128,4096]{1,0:T(8,128)(2,1)}, u32[]{:S(2)}, u32[]{:S(2)}) %collective-permute-start.15) | collective-permute-done | bytes 1048608 | tf_op jit(solution)/shard_map/ppermute | solution.py:116
  100.5 3.6 %fusion.27 = f32[128,448]{0,1:T(8,128)S(1)} fusion(bf16[128,4096]{1,0:T(8,128)(2,1)} %collective-permute-done.15, bf16[4096,224]{0,1:T(8,128)(2,1)} %copy-done.4, bf16[4096,224]{0,1:T(8,128)(2,1)} %copy-done.2), kind=kOutput, calls=%fused_computation.97 | convolution fusion | flops 477102080 | bytes 4947968 | tf_op jit(solution)/shard_map/dot_general | solution.py:390
  106.5 11.9 %collective-permute-done.21 = bf16[128,4096]{1,0:T(8,128)(2,1)} collective-permute-done((bf16[128,4096]{1,0:T(8,128)(2,1)}, bf16[128,4096]{1,0:T(8,128)(2,1)}, u32[]{:S(2)}, u32[]{:S(2)}) %collective-permute-start.21) | collective-permute-done | bytes 1048608 | tf_op jit(solution)/shard_map/ppermute | solution.py:116
  130.2 3.8 %collective-permute-start.17 = (bf16[64,448]{1,0:T(8,128)(2,1)}, bf16[64,448]{1,0:T(8,128)(2,1)S(1)}, u32[]{:S(2)}, u32[]{:S(2)}) collective-permute-start(bf16[64,448]{1,0:T(8,128)(2,1)} %add_convert_fusion.13), channel_id=1, source_target_pairs={{0,12},{2,14},{4,0},{6,2},{8,4},{10,6},{12,8},{14,10},{1,13},{3,15... | collective-permute-start | bytes 172040 | tf_op jit(solution)/shard_map/ppermute | solution.py:133
  134.0 9.7 %collective-permute-done.27 = bf16[128,4096]{1,0:T(8,128)(2,1)} collective-permute-done((bf16[128,4096]{1,0:T(8,128)(2,1)}, bf16[128,4096]{1,0:T(8,128)(2,1)}, u32[]{:S(2)}, u32[]{:S(2)}) %collective-permute-start.27) | collective-permute-done | bytes 1048608 | tf_op jit(solution)/shard_map/ppermute | solution.py:116
  149.7 3.7 %fusion.23 = f32[128,448]{0,1:T(8,128)} fusion(bf16[128,4096]{1,0:T(8,128)(2,1)} %collective-permute-done.27, bf16[4096,224]{0,1:T(8,128)(2,1)} %copy-done.4, bf16[4096,224]{0,1:T(8,128)(2,1)S(1)} %copy-done.3), kind=kOutput, calls=%fused_computation.93 | convolution fusion | flops 477102080 | bytes 4947968 | tf_op jit(solution)/shard_map/dot_general | solution.py:390
  155.7 4.4 %collective-permute-start.20 = (bf16[64,448]{1,0:T(8,128)(2,1)}, bf16[64,448]{1,0:T(8,128)(2,1)S(1)}, u32[]{:S(2)}, u32[]{:S(2)}) collective-permute-start(bf16[64,448]{1,0:T(8,128)(2,1)} %add_convert_fusion.12), channel_id=1, source_target_pairs={{0,14},{2,12},{4,2},{6,0},{8,6},{10,4},{12,10},{14,8},{1,15},{3,13... | collective-permute-start | bytes 172040 | tf_op jit(solution)/shard_map/ppermute | solution.py:133
  160.7 7.4 %collective-permute-done.30 = bf16[128,4096]{1,0:T(8,128)(2,1)} collective-permute-done((bf16[128,4096]{1,0:T(8,128)(2,1)}, bf16[128,4096]{1,0:T(8,128)(2,1)}, u32[]{:S(2)}, u32[]{:S(2)}) %collective-permute-start.30) | collective-permute-done | bytes 1048608 | tf_op jit(solution)/shard_map/ppermute | solution.py:120
  181.1 6.2 %collective-permute-done.26.refs_5_ = bf16[64,448]{1,0:T(8,128)(2,1)S(1)} collective-permute-done((bf16[64,448]{1,0:T(8,128)(2,1)}, bf16[64,448]{1,0:T(8,128)(2,1)S(1)}, u32[]{:S(2)}, u32[]{:S(2)}) %collective-permute-start.26) | collective-permute-done | bytes 57376 | tf_op jit(solution)/shard_map/ppermute | solution.py:133
  189.6 12.7 %collective-permute-done.33.refs_0_ = bf16[64,3584]{1,0:T(8,128)(2,1)S(1)} collective-permute-done((bf16[64,3584]{1,0:T(8,128)(2,1)S(1)}, bf16[64,3584]{1,0:T(8,128)(2,1)S(1)}, u32[]{:S(2)}, u32[]{:S(2)}) %collective-permute-start.33) | collective-permute-done | bytes 458784 | tf_op jit(solution)/shard_map/ppermute | solution.py:116
  203.8 11.4 %collective-permute-done.41.refs_0_ = bf16[64,3584]{1,0:T(8,128)(2,1)S(1)} collective-permute-done((bf16[64,3584]{1,0:T(8,128)(2,1)S(1)}, bf16[64,3584]{1,0:T(8,128)(2,1)S(1)}, u32[]{:S(2)}, u32[]{:S(2)}) %collective-permute-start.41) | collective-permute-done | bytes 458784 | tf_op jit(solution)/shard_map/ppermute | solution.py:116
  218.3 11.3 %expert.7 = (bf16[64,3584]{1,0:T(8,128)(2,1)S(1)}, bf16[64,3584]{1,0:T(8,128)(2,1)S(1)}, bf16[64,3584]{1,0:T(8,128)(2,1)S(1)}, bf16[64,3584]{1,0:T(8,128)(2,1)S(1)}) custom-call(f32[256,1]{1,0:T(8,128)S(1)} %copy.112.share, bf16[1,3584,1024]{2,1,0:T(8,128)(2,1)S(1)} %copy-done, bf16[1,3584,1024]{2,1,0:T(8,128)(2,1)} %up_w.7, bf16[1,1024,3584]{2,1,0:T(8,128)(2,1)} %down_w.7, ...), custom_call_target="tpu_custom_call" | custom-call | flops 5637144576 | bytes 27262976 | tf_op jit(solution)/shard_map/expert/pallas_call | solution.py:306
  233.9 11.1 %expert.4 = (bf16[64,3584]{1,0:T(8,128)(2,1)S(1)}, bf16[64,3584]{1,0:T(8,128)(2,1)S(1)}, bf16[64,3584]{1,0:T(8,128)(2,1)S(1)}, bf16[64,3584]{1,0:T(8,128)(2,1)S(1)}) custom-call(f32[256,1]{1,0:T(8,128)S(1)} %copy.109.share, bf16[1,3584,1024]{2,1,0:T(8,128)(2,1)S(1)} %copy-done.1, bf16[1,3584,1024]{2,1,0:T(8,128)(2,1)} %up_w.7, ...), custom_call_target="tpu_custom_call" | custom-call | flops 5637144576 | bytes 27262976 | tf_op jit(solution)/shard_map/expert/pallas_call | solution.py:306
  247.6 11.1 %expert.5 = (bf16[64,3584]{1,0:T(8,128)(2,1)S(1)}, bf16[64,3584]{1,0:T(8,128)(2,1)S(1)}, bf16[64,3584]{1,0:T(8,128)(2,1)S(1)}, bf16[64,3584]{1,0:T(8,128)(2,1)S(1)}) custom-call(f32[256,1]{1,0:T(8,128)S(1)} %copy.110.share, bf16[1,3584,1024]{2,1,0:T(8,128)(2,1)S(1)} %copy-done.1, bf16[1,3584,1024]{2,1,0:T(8,128)(2,1)} %up_w.7, ...), custom_call_target="tpu_custom_call" | custom-call | flops 5637144576 | bytes 27262976 | tf_op jit(solution)/shard_map/expert/pallas_call | solution.py:306
  263.0 11.1 %expert.6 = (bf16[64,3584]{1,0:T(8,128)(2,1)S(1)}, bf16[64,3584]{1,0:T(8,128)(2,1)S(1)}, bf16[64,3584]{1,0:T(8,128)(2,1)S(1)}, bf16[64,3584]{1,0:T(8,128)(2,1)S(1)}) custom-call(f32[256,1]{1,0:T(8,128)S(1)} %copy.111.share, bf16[1,3584,1024]{2,1,0:T(8,128)(2,1)S(1)} %copy-done.1, bf16[1,3584,1024]{2,1,0:T(8,128)(2,1)} %up_w.7, ...), custom_call_target="tpu_custom_call" | custom-call | flops 5637144576 | bytes 27262976 | tf_op jit(solution)/shard_map/expert/pallas_call | solution.py:306
  276.3 10.8 %collective-permute-done.47 = bf16[64,3584]{1,0:T(8,128)(2,1)S(1)} collective-permute-done((bf16[64,3584]{1,0:T(8,128)(2,1)S(1)}, bf16[64,3584]{1,0:T(8,128)(2,1)S(1)}, u32[]{:S(2)}, u32[]{:S(2)}) %collective-permute-start.47) | collective-permute-done | bytes 458784 | tf_op jit(solution)/shard_map/ppermute | solution.py:120
  292.5 8.0 %collective-permute-done.55 = bf16[64,3584]{1,0:T(8,128)(2,1)S(1)} collective-permute-done((bf16[64,3584]{1,0:T(8,128)(2,1)S(1)}, bf16[64,3584]{1,0:T(8,128)(2,1)S(1)}, u32[]{:S(2)}, u32[]{:S(2)}) %collective-permute-start.55) | collective-permute-done | bytes 458784 | tf_op jit(solution)/shard_map/ppermute | solution.py:120
  300.5 4.0 %collective-permute-done.48 = bf16[64,3584]{1,0:T(8,128)(2,1)S(1)} collective-permute-done((bf16[64,3584]{1,0:T(8,128)(2,1)S(1)}, bf16[64,3584]{1,0:T(8,128)(2,1)S(1)}, u32[]{:S(2)}, u32[]{:S(2)}) %collective-permute-start.48) | collective-permute-done | bytes 458784 | tf_op jit(solution)/shard_map/ppermute | solution.py:116
  304.9 3.8 %collective-permute-done.62 = bf16[64,3584]{1,0:T(8,128)(2,1)S(1)} collective-permute-done((bf16[64,3584]{1,0:T(8,128)(2,1)S(1)}, bf16[64,3584]{1,0:T(8,128)(2,1)S(1)}, u32[]{:S(2)}, u32[]{:S(2)}) %collective-permute-start.62) | collective-permute-done | bytes 458784 | tf_op jit(solution)/shard_map/ppermute | solution.py:120
  308.7 9.0 %collective-permute-done.56 = bf16[64,3584]{1,0:T(8,128)(2,1)S(1)} collective-permute-done((bf16[64,3584]{1,0:T(8,128)(2,1)S(1)}, bf16[64,3584]{1,0:T(8,128)(2,1)S(1)}, u32[]{:S(2)}, u32[]{:S(2)}) %collective-permute-start.56) | collective-permute-done | bytes 458784 | tf_op jit(solution)/shard_map/ppermute | solution.py:116
  (225 shorter events, 101.2 us)
Async XLA Ops:
  5.2 42.3 %collective-permute-start = (bf16[32,64,288]{2,1,0:T(8,128)(2,1)}, bf16[32,64,288]{2,1,0:T(8,128)(2,1)}, u32[]{:S(2)}, u32[]{:S(2)}) collective-permute-start(bf16[32,64,288]{2,1,0:T(8,128)(2,1)} %bitcast.82), channel_id=1, source_target_pairs={{0,1},{1,0},{2,3},{3,2},{4,5},{5,4},{6,7},{7,6},{8,9},{9,8},{10,11... | collective-permute-start | bytes 3538952 | tf_op jit(solution)/shard_map/ppermute | solution.py:124
  8.8 59.9 %collective-permute-start.10 = (bf16[4096,224]{0,1:T(8,128)(2,1)}, bf16[4096,224]{0,1:T(8,128)(2,1)}, u32[]{:S(2)}, u32[]{:S(2)}) collective-permute-start(bf16[4096,224]{0,1:T(8,128)(2,1)} %constant_dynamic-slice_fusion.18), channel_id=1, source_target_pairs={{0,1},{1,0},{2,3},{3,2},{4,5},{5,4},{6,7},{7,6},{8,9},{9,8},{10,11... | collective-permute-start | bytes 5505032 | tf_op jit(solution)/shard_map/ppermute | solution.py:124
  13.0 22.5 %all-to-all-start = ((bf16[8,64,320]{2,1,0:T(8,128)(2,1)}), bf16[8,64,320]{2,1,0:T(8,128)(2,1)S(1)}, u32[]{:S(2)}, u32[]{:S(2)}) async-start(bf16[8,64,320]{2,1,0:T(8,128)(2,1)} %broadcast_in_dim.54), calls=%async_computation | async-start | bytes 786432 | tf_op jit(solution)/shard_map/all_to_all | solution.py:356
  38.9 25.8 %collective-permute-start.3 = (bf16[32,32,128]{2,1,0:T(8,128)(2,1)S(1)}, bf16[32,32,128]{2,1,0:T(8,128)(2,1)S(1)}, u32[]{:S(2)}, u32[]{:S(2)}) collective-permute-start(bf16[32,32,128]{2,1,0:T(8,128)(2,1)S(1)} %pad_maximum_fusion.1.refs_0_), channel_id=1, source_target_pairs={{0,2},{2,0},{1,3},{3,1},{4,6},{6,4},{5,7},{7,5},{8,10},{10,8},{9,1... | collective-permute-start | bytes 786440 | tf_op jit(solution)/shard_map/ppermute | solution.py:120
  39.5 25.2 %collective-permute-start.5 = (bf16[32,32,128]{2,1,0:T(8,128)(2,1)S(1)}, bf16[32,32,128]{2,1,0:T(8,128)(2,1)S(1)}, u32[]{:S(2)}, u32[]{:S(2)}) collective-permute-start(bf16[32,32,128]{2,1,0:T(8,128)(2,1)S(1)} %collective-permute-done.4.refs_2_), channel_id=1, source_target_pairs={{0,2},{2,0},{1,3},{3,1},{4,6},{6,4},{5,7},{7,5},{8,10},{10,8},{9,1... | collective-permute-start | bytes 786440 | tf_op jit(solution)/shard_map/ppermute | solution.py:120
  46.1 18.7 %collective-permute-start.7 = (bf16[32,32,128]{2,1,0:T(8,128)(2,1)S(1)}, bf16[32,32,128]{2,1,0:T(8,128)(2,1)S(1)}, u32[]{:S(2)}, u32[]{:S(2)}) collective-permute-start(bf16[32,32,128]{2,1,0:T(8,128)(2,1)S(1)} %collective-permute-done.6.refs_4_), channel_id=1, source_target_pairs={{0,2},{2,0},{1,3},{3,1},{4,6},{6,4},{5,7},{7,5},{8,10},{10,8},{9,1... | collective-permute-start | bytes 786440 | tf_op jit(solution)/shard_map/ppermute | solution.py:120
  47.5 17.2 %collective-permute-start.9 = (bf16[32,32,128]{2,1,0:T(8,128)(2,1)S(1)}, bf16[32,32,128]{2,1,0:T(8,128)(2,1)S(1)}, u32[]{:S(2)}, u32[]{:S(2)}) collective-permute-start(bf16[32,32,128]{2,1,0:T(8,128)(2,1)S(1)} %collective-permute-done.8.refs_6_), channel_id=1, source_target_pairs={{0,2},{2,0},{1,3},{3,1},{4,6},{6,4},{5,7},{7,5},{8,10},{10,8},{9,1... | collective-permute-start | bytes 786440 | tf_op jit(solution)/shard_map/ppermute | solution.py:120
  66.7 26.2 %collective-permute-start.15 = (bf16[128,4096]{1,0:T(8,128)(2,1)S(1)}, bf16[128,4096]{1,0:T(8,128)(2,1)}, u32[]{:S(2)}, u32[]{:S(2)}) collective-permute-start(bf16[128,4096]{1,0:T(8,128)(2,1)S(1)} %raise_values.1), channel_id=1, source_target_pairs={{0,4},{4,8},{8,12},{12,0},{1,5},{5,9},{9,13},{13,1},{2,6},{6,10},{... | collective-permute-start | bytes 3145736 | tf_op jit(solution)/shard_map/ppermute | solution.py:116
  67.1 28.9 %collective-permute-start.12 = (bf16[128,4096]{1,0:T(8,128)(2,1)S(1)}, bf16[128,4096]{1,0:T(8,128)(2,1)}, u32[]{:S(2)}, u32[]{:S(2)}) collective-permute-start(bf16[128,4096]{1,0:T(8,128)(2,1)S(1)} %raise_values.1), channel_id=1, source_target_pairs={{0,2},{2,0},{1,3},{3,1},{4,6},{6,4},{5,7},{7,5},{8,10},{10,8},{9,1... | collective-permute-start | bytes 3145736 | tf_op jit(solution)/shard_map/ppermute | solution.py:120
  92.9 25.4 %collective-permute-start.21 = (bf16[128,4096]{1,0:T(8,128)(2,1)}, bf16[128,4096]{1,0:T(8,128)(2,1)}, u32[]{:S(2)}, u32[]{:S(2)}) collective-permute-start(bf16[128,4096]{1,0:T(8,128)(2,1)} %collective-permute-done.15), channel_id=1, source_target_pairs={{0,4},{4,8},{8,12},{12,0},{1,5},{5,9},{9,13},{13,1},{2,6},{6,10},{... | collective-permute-start | bytes 3145736 | tf_op jit(solution)/shard_map/ppermute | solution.py:116
  94.4 81.0 %collective-permute-start.11 = (bf16[64,448]{1,0:T(8,128)(2,1)S(1)}, bf16[64,448]{1,0:T(8,128)(2,1)S(1)}, u32[]{:S(2)}, u32[]{:S(2)}) collective-permute-start(bf16[64,448]{1,0:T(8,128)(2,1)S(1)} %copy.116), channel_id=1, source_target_pairs={{0,1},{1,0},{2,3},{3,2},{4,5},{5,4},{6,7},{7,6},{8,9},{9,8},{10,11... | collective-permute-start | bytes 172040 | tf_op jit(solution)/shard_map/ppermute | solution.py:124
  94.5 26.3 %collective-permute-start.18 = (bf16[128,4096]{1,0:T(8,128)(2,1)}, bf16[128,4096]{1,0:T(8,128)(2,1)}, u32[]{:S(2)}, u32[]{:S(2)}) collective-permute-start(bf16[128,4096]{1,0:T(8,128)(2,1)} %collective-permute-done.15), channel_id=1, source_target_pairs={{0,2},{2,0},{1,3},{3,1},{4,6},{6,4},{5,7},{7,5},{8,10},{10,8},{9,1... | collective-permute-start | bytes 3145736 | tf_op jit(solution)/shard_map/ppermute | solution.py:120
  105.9 72.0 %collective-permute-start.14 = (bf16[64,448]{1,0:T(8,128)(2,1)S(1)}, bf16[64,448]{1,0:T(8,128)(2,1)S(1)}, u32[]{:S(2)}, u32[]{:S(2)}) collective-permute-start(bf16[64,448]{1,0:T(8,128)(2,1)S(1)} %add_convert_fusion.14), channel_id=1, source_target_pairs={{0,2},{2,0},{4,6},{6,4},{8,10},{10,8},{12,14},{14,12},{1,3},{3,1},... | collective-permute-start | bytes 172040 | tf_op jit(solution)/shard_map/ppermute | solution.py:133
  118.3 25.4 %collective-permute-start.27 = (bf16[128,4096]{1,0:T(8,128)(2,1)}, bf16[128,4096]{1,0:T(8,128)(2,1)}, u32[]{:S(2)}, u32[]{:S(2)}) collective-permute-start(bf16[128,4096]{1,0:T(8,128)(2,1)} %collective-permute-done.21), channel_id=1, source_target_pairs={{0,4},{4,8},{8,12},{12,0},{1,5},{5,9},{9,13},{13,1},{2,6},{6,10},{... | collective-permute-start | bytes 3145736 | tf_op jit(solution)/shard_map/ppermute | solution.py:116
  119.0 26.8 %collective-permute-start.24 = (bf16[128,4096]{1,0:T(8,128)(2,1)}, bf16[128,4096]{1,0:T(8,128)(2,1)}, u32[]{:S(2)}, u32[]{:S(2)}) collective-permute-start(bf16[128,4096]{1,0:T(8,128)(2,1)} %collective-permute-done.21), channel_id=1, source_target_pairs={{0,2},{2,0},{1,3},{3,1},{4,6},{6,4},{5,7},{7,5},{8,10},{10,8},{9,1... | collective-permute-start | bytes 3145736 | tf_op jit(solution)/shard_map/ppermute | solution.py:120
  130.2 49.2 %collective-permute-start.17 = (bf16[64,448]{1,0:T(8,128)(2,1)}, bf16[64,448]{1,0:T(8,128)(2,1)S(1)}, u32[]{:S(2)}, u32[]{:S(2)}) collective-permute-start(bf16[64,448]{1,0:T(8,128)(2,1)} %add_convert_fusion.13), channel_id=1, source_target_pairs={{0,12},{2,14},{4,0},{6,2},{8,4},{10,6},{12,8},{14,10},{1,13},{3,15... | collective-permute-start | bytes 172040 | tf_op jit(solution)/shard_map/ppermute | solution.py:133
  143.7 24.4 %collective-permute-start.30 = (bf16[128,4096]{1,0:T(8,128)(2,1)}, bf16[128,4096]{1,0:T(8,128)(2,1)}, u32[]{:S(2)}, u32[]{:S(2)}) collective-permute-start(bf16[128,4096]{1,0:T(8,128)(2,1)} %collective-permute-done.27), channel_id=1, source_target_pairs={{0,2},{2,0},{1,3},{3,1},{4,6},{6,4},{5,7},{7,5},{8,10},{10,8},{9,1... | collective-permute-start | bytes 3145736 | tf_op jit(solution)/shard_map/ppermute | solution.py:120
  155.7 24.1 %collective-permute-start.20 = (bf16[64,448]{1,0:T(8,128)(2,1)}, bf16[64,448]{1,0:T(8,128)(2,1)S(1)}, u32[]{:S(2)}, u32[]{:S(2)}) collective-permute-start(bf16[64,448]{1,0:T(8,128)(2,1)} %add_convert_fusion.12), channel_id=1, source_target_pairs={{0,14},{2,12},{4,2},{6,0},{8,6},{10,4},{12,10},{14,8},{1,15},{3,13... | collective-permute-start | bytes 172040 | tf_op jit(solution)/shard_map/ppermute | solution.py:133
  189.5 25.7 %collective-permute-start.58 = (bf16[64,3584]{1,0:T(8,128)(2,1)S(1)}, bf16[64,3584]{1,0:T(8,128)(2,1)}, u32[]{:S(2)}, u32[]{:S(2)}) collective-permute-start(bf16[64,3584]{1,0:T(8,128)(2,1)S(1)} %get-tuple-element.25.refs_0_), channel_id=1, source_target_pairs={{0,1},{1,0},{2,3},{3,2},{4,5},{5,4},{6,7},{7,6},{8,9},{9,8},{10,11... | collective-permute-start | bytes 1376264 | tf_op jit(solution)/shard_map/ppermute | solution.py:124
  203.3 27.0 %collective-permute-start.35 = (bf16[64,3584]{1,0:T(8,128)(2,1)S(1)}, bf16[64,3584]{1,0:T(8,128)(2,1)S(1)}, u32[]{:S(2)}, u32[]{:S(2)}) collective-permute-start(bf16[64,3584]{1,0:T(8,128)(2,1)S(1)} %collective-permute-done.33.refs_0_), channel_id=1, source_target_pairs={{0,1},{1,0},{2,3},{3,2},{4,5},{5,4},{6,7},{7,6},{8,9},{9,8},{10,11... | collective-permute-start | bytes 1376264 | tf_op jit(solution)/shard_map/ppermute | solution.py:124
  229.6 61.2 %collective-permute-start.61 = (bf16[64,3584]{1,0:T(8,128)(2,1)S(1)}, bf16[64,3584]{1,0:T(8,128)(2,1)S(1)}, u32[]{:S(2)}, u32[]{:S(2)}) collective-permute-start(bf16[64,3584]{1,0:T(8,128)(2,1)S(1)} %get-tuple-element.41), channel_id=1, source_target_pairs={{0,1},{1,0},{2,3},{3,2},{4,5},{5,4},{6,7},{7,6},{8,9},{9,8},{10,11... | collective-permute-start | bytes 1376264 | tf_op jit(solution)/shard_map/ppermute | solution.py:124
  230.2 74.7 %collective-permute-start.60 = (bf16[64,3584]{1,0:T(8,128)(2,1)S(1)}, bf16[64,3584]{1,0:T(8,128)(2,1)S(1)}, u32[]{:S(2)}, u32[]{:S(2)}) collective-permute-start(bf16[64,3584]{1,0:T(8,128)(2,1)S(1)} %get-tuple-element.39), channel_id=1, source_target_pairs={{0,1},{1,0},{2,3},{3,2},{4,5},{5,4},{6,7},{7,6},{8,9},{9,8},{10,11... | collective-permute-start | bytes 1376264 | tf_op jit(solution)/shard_map/ppermute | solution.py:124
  245.5 28.5 %collective-permute-start.37 = (bf16[64,3584]{1,0:T(8,128)(2,1)S(1)}, bf16[64,3584]{1,0:T(8,128)(2,1)S(1)}, u32[]{:S(2)}, u32[]{:S(2)}) collective-permute-start(bf16[64,3584]{1,0:T(8,128)(2,1)S(1)} %get-tuple-element.27), channel_id=1, source_target_pairs={{0,1},{1,0},{2,3},{3,2},{4,5},{5,4},{6,7},{7,6},{8,9},{9,8},{10,11... | collective-permute-start | bytes 1376264 | tf_op jit(solution)/shard_map/ppermute | solution.py:124
  291.0 17.8 %collective-permute-start.62 = (bf16[64,3584]{1,0:T(8,128)(2,1)S(1)}, bf16[64,3584]{1,0:T(8,128)(2,1)S(1)}, u32[]{:S(2)}, u32[]{:S(2)}) collective-permute-start(bf16[64,3584]{1,0:T(8,128)(2,1)S(1)} %add_convert_fusion.1), channel_id=1, source_target_pairs={{0,2},{2,0},{1,3},{3,1},{4,6},{6,4},{5,7},{7,5},{8,10},{10,8},{9,1... | collective-permute-start | bytes 1376264 | tf_op jit(solution)/shard_map/ppermute | solution.py:120
  (51 other events, 518.8 us)
